TPU v7x, 512 devices: a whole 4x4x16 slice. The times are simulated.
512 devices in a mesh: dp: 64 (over x, z_hi, y, core), fsdp: 8 (over z_lo).
Axes of the slice: x: 4, y: 4, z: 16 (z_hi: 2, z_lo: 8; z = z_hi * 8 + z_lo), core: 2. Of those that a mesh axis runs over, the one named last changes fastest.
Arguments:
- inputs: bfloat16 [49152, 8192], P('dp', 'fsdp'), may hold values from -6 to 6
- grad_out: bfloat16 [49152, 14336], P('dp', 'fsdp'), may hold values from -0.078125 to 0.078125
- projector: bfloat16 [8192, 256], P('fsdp', 'dp'), may hold values from -0.0625 to 0.0625
- moment: float32 [14336, 256], P(('fsdp', 'dp')), may hold values from -3 to 3
- second: float32 [14336, 256], P(('fsdp', 'dp')), may hold values from 0.05 to 2
Outputs:
- update: bfloat16 [8, 1792, 8192], P(None, 'dp', 'fsdp')
- moment_new: float32 [14336, 256], P(('fsdp', 'dp'))
- second_new: float32 [14336, 256], P(('fsdp', 'dp'))
All inputs are finite; a program needn't handle non-finite values.
Results may differ from a plain program's by a relative error of at most 0.005.
Values may be sent and summed in bfloat16 or wider, within the bound.
A program may use at most 64 MiB of HBM per device.

v0:
```python
import jax
import jax.numpy as jnp
from jax import lax
from jax.sharding import PartitionSpec as P

STEP = 10


BETA_FIRST = 0.9
BETA_SECOND = 0.999
EPSILON = 1e-08


def adam_direction(grad_sub, moment, second):
    moment_new = BETA_FIRST * moment + (1.0 - BETA_FIRST) * grad_sub
    second_new = BETA_SECOND * second + (1.0 - BETA_SECOND) * grad_sub * grad_sub
    first_hat = moment_new / (1.0 - BETA_FIRST**STEP)
    second_hat = second_new / (1.0 - BETA_SECOND**STEP)
    direction = (first_hat / (jnp.sqrt(second_hat) + EPSILON)).astype(jnp.bfloat16)
    return (moment_new, second_new, direction)


def local(inputs, grad_out, projector, moment, second):
    full_basis = lax.all_gather(projector, "dp", axis=1, tiled=True)
    local_proj = jnp.dot(inputs, full_basis, preferred_element_type=jnp.float32)
    projected = lax.psum(local_proj, "fsdp").astype(jnp.bfloat16)
    owned_units = grad_out.shape[1] // lax.axis_size("dp")
    block_terms = lax.dot_general(
        grad_out, projected, (((0,), (0,)), ((), ())), preferred_element_type=jnp.float32
    )
    block_total = lax.psum(block_terms, "dp")
    owned_start = lax.axis_index("dp") * owned_units
    grad_sub = lax.dynamic_slice_in_dim(block_total, owned_start, owned_units, 0)
    moment_new, second_new, direction = adam_direction(grad_sub, moment, second)
    gathered = lax.all_gather(direction, "fsdp", axis=0, tiled=True)
    decoded = lax.dot_general(
        gathered, full_basis, (((1,), (1,)), ((), ())), preferred_element_type=jnp.float32
    )
    blocks = lax.axis_size("fsdp")
    update = decoded.astype(jnp.bfloat16).reshape(blocks, owned_units, decoded.shape[1])
    return (update, moment_new, second_new)


def solution(mesh):
    return jax.shard_map(
        local,
        mesh=mesh,
        in_specs=(
            P("dp", "fsdp"),
            P("dp", "fsdp"),
            P("fsdp", "dp"),
            P(("fsdp", "dp"), None),
            P(("fsdp", "dp"), None),
        ),
        out_specs=(P(None, "dp", "fsdp"), P(("fsdp", "dp"), None), P(("fsdp", "dp"), None)),
        check_vma=False,
    )
```

profile of v0, /device:TPU:32, one launch (start us, length us, event | category | flops | bytes accessed | tf_op | source)
XLA Modules:
  0.0 1367.8 jit_solution(3567450988794486704)
XLA Ops:
  7.2 0.0 copy-start
  7.2 0.0 all-reduce.3.cloned.1.call-start
  7.2 170.6 %all-gather = bf16[64,4,1024]{2,1,0:T(4,128)(2,1)} all-gather(bf16[1,4,1024]{2,1,0:T(4,128)(2,1)} %bitcast.13), channel_id=1, replica_groups=mesh['dp'=64,'fsdp'=8] {'dp'}, dimensions={0}, use_global_device_ids=true | all-gather | bytes 532480 | tf_op jit(solution)/shard_map/all_gather | solution.py:24
  177.8 1.2 reshape.11
  179.0 2.9 fusion.4
  181.9 57.4 %all-reduce.4 = bf16[768,256]{1,0:T(8,128)(2,1)} all-reduce(f32[768,256]{1,0:T(8,128)} %fusion.4), channel_id=1, replica_groups=mesh['dp'=64,'fsdp'=8] {'fsdp'}, use_global_device_ids=true, to_apply=%region_0.0 | all-reduce | flops 196608 | bytes 1179648 | tf_op jit(solution)/shard_map/psum | solution.py:26
  239.3 0.0 copy-done
  239.3 3.4 convolution_bitcast_fusion
  242.7 0.0 copy-start.1
  242.7 0.0 copy-start.2
  242.7 0.0 all-reduce.3.cloned.1.call-update
  242.7 1066.7 %all-reduce.3.cloned.1.call-done = f32[1792,256]{1,0:T(8,128)} async-done(((f32[1792,256]{1,0:T(8,128)}), f32[1792,256]{1,0:T(8,128)}) %all-reduce.3.cloned.1.call-update) | async-done | bytes 1835024 | tf_op jit(solution)/shard_map/psum | solution.py:31
  1309.4 0.0 copy-done.1
  1309.5 0.0 copy-done.2
  1309.5 1.4 fusion.2
  1310.9 46.9 %all-gather.1 = bf16[8,28,256]{2,1,0:T(8,128)(2,1)S(1)} all-gather(bf16[1,28,256]{2,1,0:T(8,128)(2,1)S(1)} %get-tuple-element.15), channel_id=1, replica_groups=mesh['dp'=64,'fsdp'=8] {'fsdp'}, dimensions={0}, use_global_device_ids=true | all-gather | bytes 129024 | tf_op jit(solution)/shard_map/all_gather | solution.py:35
  1357.8 1.1 convolution_convert_fusion
  1358.8 1.1 reshape.9
  1360.0 1.0 copy.26
  (1 shorter events, 0.0 us)
Async XLA Ops:
  7.2 232.2 %copy-start = (bf16[768,1792]{1,0:T(8,128)(2,1)S(1)}, bf16[768,1792]{1,0:T(8,128)(2,1)}, u32[]{:S(2)}) copy-start(bf16[768,1792]{1,0:T(8,128)(2,1)} %param.6) | copy-start | bytes 8257540
  7.2 1302.3 %all-reduce.3.cloned.1.call-start = ((), (), s32[]{:S(2)}) async-start(), calls=%async_computation | async-start | bytes 3670016 | tf_op jit(solution)/shard_map/psum | solution.py:31
  242.7 1066.7 %copy-start.1 = (f32[28,256]{1,0:T(8,128)S(1)}, f32[28,256]{1,0:T(8,128)}, u32[]{:S(2)}) copy-start(f32[28,256]{1,0:T(8,128)} %param.8) | copy-start | bytes 86020
  242.7 1066.7 %copy-start.2 = (f32[28,256]{1,0:T(8,128)S(1)}, f32[28,256]{1,0:T(8,128)}, u32[]{:S(2)}) copy-start(f32[28,256]{1,0:T(8,128)} %param.9) | copy-start | bytes 86020
Sparse Core Ops, SparseCore 0:
  242.9 1066.5 all-reduce.2
where the time goes:
time: 1370 us
  waiting for transfers between devices  1070 us (78%)
  blocking collectives  275 us (20%)
  between operations  14.1 us (1%)
    psum x1, waiting for transfers between devices, local(): block_total = lax.psum(block_terms, 'dp')  1070 us
    all_gather x1, blocking collectives, local(): full_basis = lax.all_gather(projector, 'dp', axis=1, tiled=True)  171 us
    psum x1, blocking collectives, local(): projected = lax.psum(local_proj, 'fsdp').astype(jnp.bfloat16)  57.4 us
    all_gather x1, blocking collectives, local(): gathered = lax.all_gather(direction, 'fsdp', axis=0, tiled=True)  46.9 us
  transfers between devices with their start and end apart: 1, of which 1 were waited for; matrix products, arithmetic and copies ran while one was open for 0% of the time, Pallas kernels for 0%

commit v1 on v0

v1 whole, which is shorter than its diff:
```python
import functools

import jax
import jax.numpy as jnp
from jax import lax
from jax.experimental import pallas as pl
from jax.experimental.pallas import tpu as pltpu
from jax.sharding import PartitionSpec as P

MESH = pl.DeviceIdType.MESH
F32 = jnp.float32
BF16 = jnp.bfloat16

STEP = 10
BETA_FIRST = 0.9
BETA_SECOND = 0.999
EPSILON = 1e-08

TOKENS = 768
FEATURES = 1024
UNITS = 1792
RANK = 256
OWNED = 28
PAD = 32
LINE = 8
PIECE = 48
PIECES = TOKENS // PIECE
SKEW = 6


def adam_direction(grad_sub, moment, second):
    moment_new = BETA_FIRST * moment + (1.0 - BETA_FIRST) * grad_sub
    second_new = BETA_SECOND * second + (1.0 - BETA_SECOND) * grad_sub * grad_sub
    first_hat = moment_new / (1.0 - BETA_FIRST**STEP)
    second_hat = second_new / (1.0 - BETA_SECOND**STEP)
    direction = first_hat / (jnp.sqrt(second_hat) + EPSILON)
    return (moment_new, second_new, direction)


def to_natural(v):
    return jnp.concatenate([v[:, zh * 128 + x * 32 : zh * 128 + x * 32 + 32] for x in range(4) for zh in range(2)], axis=1)


def to_halves(v):
    return jnp.concatenate([v[:, x * 64 + zh * 32 : x * 64 + zh * 32 + 32] for zh in range(2) for x in range(4)], axis=1)


def kernel(
    blk, x_hbm, go_hbm, mom, sec,
    upd, mnew, snew,
    x_v, go_v, got, raw, basis, own, pre, suf, out_r, out_l, proj, btf, btb, cbuf, s1, rb, zsend, zrecv, dirs,
    load_sem, z_send, z_recv, g_send, g_recv, c_send, c_recv, r_send, r_recv, l_send, l_recv, b_send, b_recv, d_send, d_recv,
):
    d = lax.axis_index("dp")
    f = lax.axis_index("fsdp")
    core = lax.rem(d, 2)
    y = lax.rem(d // 2, 4)
    zh = lax.rem(d // 8, 2)
    xx = d // 16
    pos = xx * 4 + y
    other_core = (d + 1 - 2 * core, f)
    other_zh = (d + 8 - 16 * zh, f)

    def at_pos(q):
        return (((q // 4) * 2 + zh) * 8 + lax.rem(q, 4) * 2 + core, f)

    load_x = pltpu.make_async_copy(x_hbm, x_v, load_sem.at[0])
    load_go = pltpu.make_async_copy(go_hbm, go_v, load_sem.at[1])
    load_x.start()
    load_go.start()

    barrier = pltpu.get_barrier_semaphore()
    pl.semaphore_signal(barrier, inc=1, device_id=other_zh, device_id_type=MESH)
    pl.semaphore_signal(barrier, inc=1, device_id=other_core, device_id_type=MESH)

    def greet(i, _):
        pl.semaphore_signal(barrier, inc=1, device_id=at_pos(lax.rem(pos + i, 16)), device_id_type=MESH)
        return 0

    lax.fori_loop(1, 16, greet, 0)

    def greet_line(i, _):
        pl.semaphore_signal(barrier, inc=1, device_id=(d, lax.rem(f + i, LINE)), device_id_type=MESH)
        return 0

    lax.fori_loop(1, LINE, greet_line, 0)
    raw[zh, core, pos] = blk[...]
    pl.semaphore_wait(barrier, 24)

    def send_block(which, i):
        q = lax.rem(pos + i, 16)
        return pltpu.make_async_remote_copy(
            raw.at[which, core, pos], raw.at[which, core, pos], g_send.at[which, i], g_recv.at[which, pos],
            device_id=at_pos(q), device_id_type=MESH)

    def wait_block(which, i):
        q = lax.rem(pos + 16 - i, 16)
        pltpu.make_async_remote_copy(
            raw.at[which, core, q], raw.at[which, core, q], g_send.at[which, i], g_recv.at[which, q],
            device_id=at_pos(q), device_id_type=MESH).wait_recv()

    def each_peer(action):
        def body(i, _):
            action(i)
            return 0
        lax.fori_loop(1, 16, body, 0)

    swap_zh = pltpu.make_async_remote_copy(
        raw.at[zh, core, pos], raw.at[zh, core, pos], z_send.at[0], z_recv.at[0], device_id=other_zh, device_id_type=MESH)
    swap_zh.start()
    each_peer(lambda i: send_block(zh, i).start())

    def swap_core(which):
        return pltpu.make_async_remote_copy(
            raw.at[which, core], raw.at[which, core], c_send.at[which], c_recv.at[which],
            device_id=other_core, device_id_type=MESH)

    load_go.wait()

    def turn(i, _):
        cols = pl.ds(pl.multiple_of(i * 128, 128), 128)
        got[cols, :] = go_v[:, cols].T
        return 0

    lax.fori_loop(0, UNITS // 128, turn, 0)

    each_peer(lambda i: wait_block(zh, i))
    swap_core(zh).start()
    swap_zh.wait_recv()
    each_peer(lambda i: send_block(1 - zh, i).start())

    row = lax.broadcasted_iota(jnp.int32, (256, 256), 0)
    col = lax.broadcasted_iota(jnp.int32, (256, 256), 1)
    source = ((row // 4) % 2) * 128 + ((row // 8) % 4) * 32 + (row // 32) * 4 + row % 4
    perm = jnp.where(col == source, 1.0, 0.0).astype(BF16)

    def unfold(which):
        for x in range(4):
            blocks = jnp.concatenate(
                [raw[which, 0, 4 * x : 4 * x + 4].reshape(128, 128), raw[which, 1, 4 * x : 4 * x + 4].reshape(128, 128)], axis=0)
            placed = jnp.dot(perm, blocks, preferred_element_type=F32).astype(BF16)
            for b in range(8):
                basis[which, 32 * x : 32 * x + 32, 128 * b : 128 * b + 128] = placed[32 * b : 32 * b + 32]

    def project(which):
        half = pl.ds(pl.multiple_of(which * 128, 128), 128)
        own[:, half] = lax.dot_general(
            x_v[...], basis[which], (((1,), (1,)), ((), ())), preferred_element_type=F32)

    load_x.wait()
    swap_core(zh).wait()
    unfold(zh)
    project(zh)
    each_peer(lambda i: wait_block(1 - zh, i))
    swap_core(1 - zh).start()
    swap_core(1 - zh).wait()
    unfold(1 - zh)
    project(1 - zh)
    swap_zh.wait_send()
    each_peer(lambda i: send_block(zh, i).wait_send())
    each_peer(lambda i: send_block(1 - zh, i).wait_send())

    @pl.when(f == 0)
    def _():
        pre[...] = jnp.zeros_like(pre)

    @pl.when(f == LINE - 1)
    def _():
        suf[...] = jnp.zeros_like(suf)

    def right(p):
        rows = pl.ds(pl.multiple_of(p * PIECE, PIECE), PIECE)
        return pltpu.make_async_remote_copy(
            out_r.at[rows], pre.at[rows], r_send.at[p], r_recv.at[p],
            device_id=(d, lax.rem(f + 1, LINE)), device_id_type=MESH)

    def left(p):
        rows = pl.ds(pl.multiple_of(p * PIECE, PIECE), PIECE)
        return pltpu.make_async_remote_copy(
            out_l.at[rows], suf.at[rows], l_send.at[p], l_recv.at[p],
            device_id=(d, lax.rem(f + LINE - 1, LINE)), device_id_type=MESH)

    def step(t, _):
        p = t - f * SKEW

        @pl.when((p >= 0) & (p < PIECES))
        def _():
            @pl.when(f > 0)
            def _():
                right(p).wait_recv()

            @pl.when(f < LINE - 1)
            def _():
                rows = pl.ds(pl.multiple_of(p * PIECE, PIECE), PIECE)
                out_r[rows] = (own[rows] + pre[rows].astype(F32)).astype(BF16)
                right(p).start()

        q = t - (LINE - 1 - f) * SKEW

        @pl.when((q >= 0) & (q < PIECES))
        def _():
            @pl.when(f < LINE - 1)
            def _():
                left(q).wait_recv()

            @pl.when(f > 0)
            def _():
                rows = pl.ds(pl.multiple_of(q * PIECE, PIECE), PIECE)
                out_l[rows] = (own[rows] + suf[rows].astype(F32)).astype(BF16)
                left(q).start()

        return 0

    lax.fori_loop(0, PIECES + (LINE - 1) * SKEW, step, 0)

    proj[...] = (own[...] + (pre[...].astype(F32) + suf[...].astype(F32))).astype(BF16)

    btf[UNITS:, :] = jnp.zeros((8, RANK), F32)

    def terms(i, _):
        rows = pl.ds(pl.multiple_of(i * 448, 448), 448)
        btf[rows, :] = jnp.dot(got[rows, :], proj[...], preferred_element_type=F32)
        return 0

    lax.fori_loop(0, UNITS // 448, terms, 0)

    def place(i, _):
        two = btf[pl.ds(pl.multiple_of(i * 56, 8), 64), :]
        j = ((i // 8) * 4 + lax.rem(i, 4)) * 2 + lax.rem(i // 4, 2)
        btb[0, j] = two[:PAD].astype(BF16)
        btb[1, j] = pltpu.roll(two, 64 - OWNED, 0)[:PAD].astype(BF16)
        return 0

    lax.fori_loop(0, 32, place, 0)

    swap_terms = pltpu.make_async_remote_copy(
        btb.at[1 - core], cbuf, c_send.at[2], c_recv.at[2], device_id=other_core, device_id_type=MESH)
    swap_terms.start()
    swap_terms.wait()

    def add_cores(i, _):
        s1[i] = (btb[core, i].astype(F32) + cbuf[i].astype(F32)).astype(BF16)
        return 0

    lax.fori_loop(0, 32, add_cores, 0)

    def send_terms(i):
        q = lax.rem(pos + i, 16)
        return pltpu.make_async_remote_copy(
            s1.at[pl.ds(q * 2, 2)], rb.at[pos], b_send.at[i], b_recv.at[pos], device_id=at_pos(q), device_id_type=MESH)

    each_peer(lambda i: send_terms(i).start())

    def add_terms(i, acc):
        q = lax.rem(pos + 16 - i, 16)
        pltpu.make_async_remote_copy(
            s1.at[pl.ds(q * 2, 2)], rb.at[q], b_send.at[i], b_recv.at[q],
            device_id=at_pos(q), device_id_type=MESH).wait_recv()
        return (acc[0] + rb[q, zh].astype(F32), acc[1] + rb[q, 1 - zh].astype(F32))

    mine, theirs = lax.fori_loop(
        1, 16, add_terms, (s1[2 * pos + zh].astype(F32), s1[2 * pos + 1 - zh].astype(F32)))
    zsend[...] = theirs.astype(BF16)
    swap_sum = pltpu.make_async_remote_copy(
        zsend, zrecv, z_send.at[1], z_recv.at[1], device_id=other_zh, device_id_type=MESH)
    swap_sum.start()
    swap_sum.wait()
    grad_sub = to_natural(mine + zrecv[...].astype(F32))

    moment_new, second_new, direction = adam_direction(grad_sub, mom[...], sec[...])
    mnew[...] = moment_new[:OWNED]
    snew[...] = second_new[:OWNED]
    dirs[f] = to_halves(direction).astype(BF16)

    def send_dir(i):
        return pltpu.make_async_remote_copy(
            dirs.at[f], dirs.at[f], d_send.at[i], d_recv.at[f],
            device_id=(d, lax.rem(f + i, LINE)), device_id_type=MESH)

    def each_line(action):
        def body(i, _):
            action(i)
            return 0
        lax.fori_loop(1, LINE, body, 0)

    each_line(lambda i: send_dir(i).start())

    def wait_dir(i):
        q = lax.rem(f + LINE - i, LINE)
        pltpu.make_async_remote_copy(
            dirs.at[q], dirs.at[q], d_send.at[i], d_recv.at[q], device_id=(d, q), device_id_type=MESH).wait_recv()

    each_line(wait_dir)
    both = basis[...].reshape(RANK, FEATURES)
    upd[...] = jnp.dot(
        dirs[...].reshape(LINE * PAD, RANK), both, preferred_element_type=F32).astype(BF16)

    each_peer(lambda i: send_terms(i).wait_send())
    each_line(lambda i: send_dir(i).wait_send())

    def sent(p, _):
        @pl.when(f < LINE - 1)
        def _():
            right(p).wait_send()

        @pl.when(f > 0)
        def _():
            left(p).wait_send()

        return 0

    lax.fori_loop(0, PIECES, sent, 0)


def local(inputs, grad_out, projector, moment, second):
    blk = projector.T.reshape(4, 8, 128).transpose(1, 0, 2).reshape(32, 128)
    grow = ((0, PAD - OWNED), (0, 0))
    vmem = pl.BlockSpec(memory_space=pltpu.VMEM)
    anywhere = pl.BlockSpec(memory_space=pl.ANY)
    dma = pltpu.SemaphoreType.DMA
    update, moment_new, second_new = pl.pallas_call(
        kernel,
        out_shape=(
            jax.ShapeDtypeStruct((LINE * PAD, FEATURES), BF16),
            jax.ShapeDtypeStruct((OWNED, RANK), F32),
            jax.ShapeDtypeStruct((OWNED, RANK), F32),
        ),
        in_specs=[vmem, anywhere, anywhere, vmem, vmem],
        out_specs=(vmem, vmem, vmem),
        scratch_shapes=[
            pltpu.VMEM((TOKENS, FEATURES), BF16),
            pltpu.VMEM((TOKENS, UNITS), BF16),
            pltpu.VMEM((UNITS, TOKENS), BF16),
            pltpu.VMEM((2, 2, 16, 32, 128), BF16),
            pltpu.VMEM((2, 128, FEATURES), BF16),
            pltpu.VMEM((TOKENS, RANK), F32),
            pltpu.VMEM((TOKENS, RANK), BF16),
            pltpu.VMEM((TOKENS, RANK), BF16),
            pltpu.VMEM((TOKENS, RANK), BF16),
            pltpu.VMEM((TOKENS, RANK), BF16),
            pltpu.VMEM((TOKENS, RANK), BF16),
            pltpu.VMEM((UNITS + 8, RANK), F32),
            pltpu.VMEM((2, 32, PAD, RANK), BF16),
            pltpu.VMEM((32, PAD, RANK), BF16),
            pltpu.VMEM((32, PAD, RANK), BF16),
            pltpu.VMEM((16, 2, PAD, RANK), BF16),
            pltpu.VMEM((PAD, RANK), BF16),
            pltpu.VMEM((PAD, RANK), BF16),
            pltpu.VMEM((LINE, PAD, RANK), BF16),
            dma((2,)),
            dma((2,)), dma((2,)),
            dma((2, 16)), dma((2, 16)),
            dma((3,)), dma((3,)),
            dma((PIECES,)), dma((PIECES,)), dma((PIECES,)), dma((PIECES,)),
            dma((16,)), dma((16,)),
            dma((LINE,)), dma((LINE,)),
        ],
        compiler_params=pltpu.CompilerParams(
            collective_id=0, has_side_effects=True, vmem_limit_bytes=48 * 1024 * 1024),
    )(blk, inputs, grad_out, jnp.pad(moment, grow), jnp.pad(second, grow, constant_values=1.0))
    return (update.reshape(LINE, PAD, FEATURES)[:, :OWNED], moment_new, second_new)


def solution(mesh):
    return jax.shard_map(
        local,
        mesh=mesh,
        in_specs=(
            P("dp", "fsdp"),
            P("dp", "fsdp"),
            P("fsdp", "dp"),
            P(("fsdp", "dp"), None),
            P(("fsdp", "dp"), None),
        ),
        out_specs=(P(None, "dp", "fsdp"), P(("fsdp", "dp"), None), P(("fsdp", "dp"), None)),
        check_vma=False,
    )
```

time: 1370 us -> 98.1 us (0.07)
  the two profiles are of different devices: /device:TPU:32 before, /device:TPU:24 now
where the time goes in v1:
time: 98.1 us; the launch traced here: 97.7 us
  Pallas kernels  89.4 us (91%)
  local copies, waits for them, and re-layouts  7.66 us (8%)
    pallas_call x1, Pallas kernels, local(): pl.pallas_call(kernel, out_shape=(jax.ShapeDtypeStruct((LINE * PAD, FEATU...  89.4 us
    unnamed x9, local copies, waits for them, and re-layouts  6.13 us

profile of v1, /device:TPU:24, one launch (start us, length us, event | category | flops | bytes accessed | tf_op | source)
XLA Modules:
  0.0 97.7 jit_solution(120225632410278708)
XLA Ops:
  0.6 0.8 pad.8.mom
  1.4 0.8 pad.9.sec
  2.2 0.0 copy-start
  2.2 1.8 %copy-done = bf16[768,1792]{1,0:T(8,128)(2,1)S(1)} copy-done((bf16[768,1792]{1,0:T(8,128)(2,1)S(1)}, bf16[768,1792]{1,0:T(8,128)(2,1)}, u32[]{:S(2)}) %copy-start) | copy-done | bytes 2752536
  3.9 0.0 copy-start.1
  3.9 1.4 %copy-done.1 = bf16[768,1024]{1,0:T(8,128)(2,1)S(1)} copy-done((bf16[768,1024]{1,0:T(8,128)(2,1)S(1)}, bf16[768,1024]{1,0:T(8,128)(2,1)}, u32[]{:S(2)}) %copy-start.1) | copy-done | bytes 1572888
  5.3 0.0 copy-start.2
  5.3 0.7 copy-done.2
  6.0 89.4 %shard_map.76 = (bf16[256,1024]{1,0:T(8,128)(2,1)S(1)}, f32[28,256]{1,0:T(8,128)S(1)}, f32[28,256]{1,0:T(8,128)S(1)}) custom-call(bf16[32,128]{1,0:T(8,128)(2,1)S(1)} %bitcast.10, bf16[768,1024]{1,0:T(8,128)(2,1)S(1)} %copy-done.1, bf16[768,1792]{1,0:T(8,128)(2,1)S(1)} %copy-done, f32[32,256]{1,0:T(8,128)S(1)} %pad.8.mom, f32[32,256]{1,0:T(8,128)S(1)} %pad.9.sec), custom_call_target="tpu_custom_call" | custom-call | tf_op jit(solution)/shard_map/pallas_call | solution.py:321
  95.5 1.0 %copy.10 = bf16[8,28,1024]{2,0,1:T(8,128)(2,1)} copy(bf16[8,28,1024]{2,1,0:T(8,128)(2,1)S(1)} %bitcast.9) | data formatting | bytes 917504
  96.5 0.6 copy.13
  97.1 0.6 copy.14
Async XLA Ops:
  2.2 1.8 %copy-start = (bf16[768,1792]{1,0:T(8,128)(2,1)S(1)}, bf16[768,1792]{1,0:T(8,128)(2,1)}, u32[]{:S(2)}) copy-start(bf16[768,1792]{1,0:T(8,128)(2,1)} %go_hbm.1) | copy-start | bytes 8257540
  3.9 1.4 %copy-start.1 = (bf16[768,1024]{1,0:T(8,128)(2,1)S(1)}, bf16[768,1024]{1,0:T(8,128)(2,1)}, u32[]{:S(2)}) copy-start(bf16[768,1024]{1,0:T(8,128)(2,1)} %x_hbm.1) | copy-start | bytes 4718596
  5.3 0.7 copy-start.2

commit v2 on v1

--- a/solution.py
+++ b/solution.py
@@ -46,10 +46,10 @@
 
 
 def kernel(
-    blk, x_hbm, go_hbm, mom, sec,
+    blk, x_hbm, go_hbm, mom_hbm, sec_hbm,
     upd, mnew, snew,
-    x_v, go_v, got, raw, basis, own, pre, suf, out_r, out_l, proj, btf, btb, cbuf, s1, rb, zsend, zrecv, dirs,
-    load_sem, z_send, z_recv, g_send, g_recv, c_send, c_recv, r_send, r_recv, l_send, l_recv, b_send, b_recv, d_send, d_recv,
+    x_v, go_v, mom, sec, got, raw, basis, own, pre, suf, out_r, out_l, proj, btf, btb, cbuf, s1, rb, zsend, zrecv, direct, dirs,
+    load_sem, z_send, z_recv, g_send, g_recv, c_send, c_recv, r_send, r_recv, l_send, l_recv, b_send, b_recv, d_send, d_recv, t_send, t_recv,
 ):
     d = lax.axis_index("dp")
     f = lax.axis_index("fsdp")
@@ -66,8 +66,12 @@
 
     load_x = pltpu.make_async_copy(x_hbm, x_v, load_sem.at[0])
     load_go = pltpu.make_async_copy(go_hbm, go_v, load_sem.at[1])
+    load_mom = pltpu.make_async_copy(mom_hbm, mom, load_sem.at[2])
+    load_sec = pltpu.make_async_copy(sec_hbm, sec, load_sem.at[3])
+    load_go.start()
     load_x.start()
-    load_go.start()
+    load_mom.start()
+    load_sec.start()
 
     barrier = pltpu.get_barrier_semaphore()
     pl.semaphore_signal(barrier, inc=1, device_id=other_zh, device_id_type=MESH)
@@ -85,6 +89,18 @@
 
     lax.fori_loop(1, LINE, greet_line, 0)
     raw[zh, core, pos] = blk[...]
+    load_go.wait()
+
+    def turn(i, _):
+        cols = pl.ds(pl.multiple_of(i * 128, 128), 128)
+        got[cols, :] = go_v[:, cols].T
+        return 0
+
+    lax.fori_loop(0, UNITS // 128, turn, 0)
+
+    load_x.wait()
+    load_mom.wait()
+    load_sec.wait()
     pl.semaphore_wait(barrier, 24)
 
     def send_block(which, i):
@@ -114,15 +130,6 @@
         return pltpu.make_async_remote_copy(
             raw.at[which, core], raw.at[which, core], c_send.at[which], c_recv.at[which],
             device_id=other_core, device_id_type=MESH)
-
-    load_go.wait()
-
-    def turn(i, _):
-        cols = pl.ds(pl.multiple_of(i * 128, 128), 128)
-        got[cols, :] = go_v[:, cols].T
-        return 0
-
-    lax.fori_loop(0, UNITS // 128, turn, 0)
 
     each_peer(lambda i: wait_block(zh, i))
     swap_core(zh).start()
@@ -147,7 +154,6 @@
         own[:, half] = lax.dot_general(
             x_v[...], basis[which], (((1,), (1,)), ((), ())), preferred_element_type=F32)
 
-    load_x.wait()
     swap_core(zh).wait()
     unfold(zh)
     project(zh)
@@ -215,46 +221,51 @@
 
     proj[...] = (own[...] + (pre[...].astype(F32) + suf[...].astype(F32))).astype(BF16)
 
-    btf[UNITS:, :] = jnp.zeros((8, RANK), F32)
+    btf[448:, :] = jnp.zeros((8, RANK), F32)
+
+    def swap_terms(x):
+        return pltpu.make_async_remote_copy(
+            btb.at[1 - core, pl.ds(x * 8, 8)], cbuf.at[pl.ds(x * 8, 8)], t_send.at[x], t_recv.at[x],
+            device_id=other_core, device_id_type=MESH)
 
     def terms(i, _):
-        rows = pl.ds(pl.multiple_of(i * 448, 448), 448)
-        btf[rows, :] = jnp.dot(got[rows, :], proj[...], preferred_element_type=F32)
-        return 0
-
-    lax.fori_loop(0, UNITS // 448, terms, 0)
-
-    def place(i, _):
-        two = btf[pl.ds(pl.multiple_of(i * 56, 8), 64), :]
-        j = ((i // 8) * 4 + lax.rem(i, 4)) * 2 + lax.rem(i // 4, 2)
-        btb[0, j] = two[:PAD].astype(BF16)
-        btb[1, j] = pltpu.roll(two, 64 - OWNED, 0)[:PAD].astype(BF16)
-        return 0
-
-    lax.fori_loop(0, 32, place, 0)
-
-    swap_terms = pltpu.make_async_remote_copy(
-        btb.at[1 - core], cbuf, c_send.at[2], c_recv.at[2], device_id=other_core, device_id_type=MESH)
-    swap_terms.start()
-    swap_terms.wait()
+        x = lax.rem(xx + 1 + i, 4)
+        first = pl.multiple_of(x * 448, 448)
+        btf[0:448, :] = jnp.dot(got[pl.ds(first, 448), :], proj[...], preferred_element_type=F32)
+        for k in range(8):
+            two = btf[56 * k : 56 * k + 64, :]
+            j = x * 8 + (k % 4) * 2 + k // 4
+            btb[0, j] = two[:PAD].astype(BF16)
+            btb[1, j] = pltpu.roll(two, 64 - OWNED, 0)[:PAD].astype(BF16)
+        swap_terms(x).start()
+        return 0
+
+    lax.fori_loop(0, 4, terms, 0)
+
+    def send_terms(q):
+        return pltpu.make_async_remote_copy(
+            s1.at[pl.ds(q * 2, 2)], rb.at[pos], b_send.at[q], b_recv.at[pos], device_id=at_pos(q), device_id_type=MESH)
 
     def add_cores(i, _):
-        s1[i] = (btb[core, i].astype(F32) + cbuf[i].astype(F32)).astype(BF16)
-        return 0
-
-    lax.fori_loop(0, 32, add_cores, 0)
-
-    def send_terms(i):
-        q = lax.rem(pos + i, 16)
-        return pltpu.make_async_remote_copy(
-            s1.at[pl.ds(q * 2, 2)], rb.at[pos], b_send.at[i], b_recv.at[pos], device_id=at_pos(q), device_id_type=MESH)
-
-    each_peer(lambda i: send_terms(i).start())
+        x = lax.rem(xx + 1 + i, 4)
+        swap_terms(x).wait()
+        for k in range(4):
+            q = x * 4 + lax.rem(y + 1 + k, 4)
+            both = pl.ds(q * 2, 2)
+            s1[both] = (btb[core, both].astype(F32) + cbuf[both].astype(F32)).astype(BF16)
+
+            @pl.when(q != pos)
+            def _():
+                send_terms(q).start()
+
+        return 0
+
+    lax.fori_loop(0, 4, add_cores, 0)
 
     def add_terms(i, acc):
         q = lax.rem(pos + 16 - i, 16)
         pltpu.make_async_remote_copy(
-            s1.at[pl.ds(q * 2, 2)], rb.at[q], b_send.at[i], b_recv.at[q],
+            s1.at[pl.ds(q * 2, 2)], rb.at[q], b_send.at[q], b_recv.at[q],
             device_id=at_pos(q), device_id_type=MESH).wait_recv()
         return (acc[0] + rb[q, zh].astype(F32), acc[1] + rb[q, 1 - zh].astype(F32))
 
@@ -265,12 +276,14 @@
         zsend, zrecv, z_send.at[1], z_recv.at[1], device_id=other_zh, device_id_type=MESH)
     swap_sum.start()
     swap_sum.wait()
-    grad_sub = to_natural(mine + zrecv[...].astype(F32))
+    grad_sub = to_natural(mine + zrecv[...].astype(F32))[:OWNED]
 
     moment_new, second_new, direction = adam_direction(grad_sub, mom[...], sec[...])
-    mnew[...] = moment_new[:OWNED]
-    snew[...] = second_new[:OWNED]
-    dirs[f] = to_halves(direction).astype(BF16)
+    mnew[...] = moment_new
+    snew[...] = second_new
+    direct[OWNED - 4 :, :] = jnp.zeros((PAD - OWNED + 4, RANK), F32)
+    direct[:OWNED, :] = to_halves(direction)
+    dirs[f] = direct[...].astype(BF16)
 
     def send_dir(i):
         return pltpu.make_async_remote_copy(
@@ -295,7 +308,7 @@
     upd[...] = jnp.dot(
         dirs[...].reshape(LINE * PAD, RANK), both, preferred_element_type=F32).astype(BF16)
 
-    each_peer(lambda i: send_terms(i).wait_send())
+    each_peer(lambda i: send_terms(lax.rem(pos + i, 16)).wait_send())
     each_line(lambda i: send_dir(i).wait_send())
 
     def sent(p, _):
@@ -314,7 +327,6 @@
 
 def local(inputs, grad_out, projector, moment, second):
     blk = projector.T.reshape(4, 8, 128).transpose(1, 0, 2).reshape(32, 128)
-    grow = ((0, PAD - OWNED), (0, 0))
     vmem = pl.BlockSpec(memory_space=pltpu.VMEM)
     anywhere = pl.BlockSpec(memory_space=pl.ANY)
     dma = pltpu.SemaphoreType.DMA
@@ -325,11 +337,13 @@
             jax.ShapeDtypeStruct((OWNED, RANK), F32),
             jax.ShapeDtypeStruct((OWNED, RANK), F32),
         ),
-        in_specs=[vmem, anywhere, anywhere, vmem, vmem],
+        in_specs=[vmem, anywhere, anywhere, anywhere, anywhere],
         out_specs=(vmem, vmem, vmem),
         scratch_shapes=[
             pltpu.VMEM((TOKENS, FEATURES), BF16),
             pltpu.VMEM((TOKENS, UNITS), BF16),
+            pltpu.VMEM((OWNED, RANK), F32),
+            pltpu.VMEM((OWNED, RANK), F32),
             pltpu.VMEM((UNITS, TOKENS), BF16),
             pltpu.VMEM((2, 2, 16, 32, 128), BF16),
             pltpu.VMEM((2, 128, FEATURES), BF16),
@@ -339,25 +353,27 @@
             pltpu.VMEM((TOKENS, RANK), BF16),
             pltpu.VMEM((TOKENS, RANK), BF16),
             pltpu.VMEM((TOKENS, RANK), BF16),
-            pltpu.VMEM((UNITS + 8, RANK), F32),
+            pltpu.VMEM((456, RANK), F32),
             pltpu.VMEM((2, 32, PAD, RANK), BF16),
             pltpu.VMEM((32, PAD, RANK), BF16),
             pltpu.VMEM((32, PAD, RANK), BF16),
             pltpu.VMEM((16, 2, PAD, RANK), BF16),
             pltpu.VMEM((PAD, RANK), BF16),
             pltpu.VMEM((PAD, RANK), BF16),
+            pltpu.VMEM((PAD, RANK), F32),
             pltpu.VMEM((LINE, PAD, RANK), BF16),
-            dma((2,)),
+            dma((4,)),
             dma((2,)), dma((2,)),
             dma((2, 16)), dma((2, 16)),
-            dma((3,)), dma((3,)),
+            dma((2,)), dma((2,)),
             dma((PIECES,)), dma((PIECES,)), dma((PIECES,)), dma((PIECES,)),
             dma((16,)), dma((16,)),
             dma((LINE,)), dma((LINE,)),
+            dma((4,)), dma((4,)),
         ],
         compiler_params=pltpu.CompilerParams(
             collective_id=0, has_side_effects=True, vmem_limit_bytes=48 * 1024 * 1024),
-    )(blk, inputs, grad_out, jnp.pad(moment, grow), jnp.pad(second, grow, constant_values=1.0))
+    )(*[pltpu.with_memory_space_constraint(v, pltpu.HBM) for v in (blk, inputs, grad_out, moment, second)])
     return (update.reshape(LINE, PAD, FEATURES)[:, :OWNED], moment_new, second_new)
 
 

time: 98.1 us -> 89.5 us (0.912)
  local copies, waits for them, and re-layouts: 7.66 us -> 2.25 us
  Pallas kernels: 89.4 us -> 86.5 us
    unnamed x9 -> x3, local copies, waits for them, and re-layouts: 6.13 us -> 2.25 us
    pallas_call x1, Pallas kernels: 89.4 us -> 86.5 us  [local(): pl.pallas_call(kernel, out_shape=(jax.ShapeDtypeStruct((LINE * PAD, FEATU...]
    pad x2 -> x0, local copies, waits for them, and re-layouts: 1.53 us -> none  [the longest x1 0.76 us: local(): jnp.pad(moment, grow)]
where the time goes in v2:
time: 89.5 us; the launch traced here: 89.4 us
  Pallas kernels  86.5 us (97%)
  local copies, waits for them, and re-layouts  2.25 us (3%)
    pallas_call x1, Pallas kernels, local(): pl.pallas_call(kernel, out_shape=(jax.ShapeDtypeStruct((LINE * PAD, FEATU...  86.5 us
    unnamed x3, local copies, waits for them, and re-layouts  2.25 us

profile of v2, /device:TPU:24, one launch (start us, length us, event | category | flops | bytes accessed | tf_op | source)
XLA Modules:
  0.0 89.4 jit_solution(6370831747417758503)
XLA Ops:
  0.6 86.5 %shard_map.76 = (bf16[256,1024]{1,0:T(8,128)(2,1)S(1)}, f32[28,256]{1,0:T(8,128)S(1)}, f32[28,256]{1,0:T(8,128)S(1)}) custom-call(bf16[32,128]{1,0:T(8,128)(2,1)} %bitcast.10, bf16[768,1024]{1,0:T(8,128)(2,1)} %x_hbm.1, bf16[768,1792]{1,0:T(8,128)(2,1)} %go_hbm.1, f32[28,256]{1,0:T(8,128)} %mom_hbm.1, f32[28,256]{1,0:T(8,128)} %sec_hbm.1), custom_call_target="tpu_custom_call" | custom-call | tf_op jit(solution)/shard_map/pallas_call | solution.py:333
  87.1 1.0 %copy.10 = bf16[8,28,1024]{2,0,1:T(8,128)(2,1)} copy(bf16[8,28,1024]{2,1,0:T(8,128)(2,1)S(1)} %bitcast.9) | data formatting | bytes 917504
  88.1 0.6 copy.13
  88.8 0.6 copy.14

commit v3 on v2

--- a/solution.py
+++ b/solution.py
@@ -23,9 +23,13 @@
 OWNED = 28
 PAD = 32
 LINE = 8
-PIECE = 48
+PIECE = 64
 PIECES = TOKENS // PIECE
-SKEW = 6
+SKEW = 9
+GATHERED = 12
+PROJECTED = 17
+LATER = 24
+ADDED = 5
 
 
 def adam_direction(grad_sub, moment, second):
@@ -48,7 +52,7 @@
 def kernel(
     blk, x_hbm, go_hbm, mom_hbm, sec_hbm,
     upd, mnew, snew,
-    x_v, go_v, mom, sec, got, raw, basis, own, pre, suf, out_r, out_l, proj, btf, btb, cbuf, s1, rb, zsend, zrecv, direct, dirs,
+    x_v, go_v, mom, sec, got, raw, basis, own, pre, suf, out_r, out_l, proj, btf, btb, cbuf, s1, rb, zsend, zrecv, total, direct, dirs,
     load_sem, z_send, z_recv, g_send, g_recv, c_send, c_recv, r_send, r_recv, l_send, l_recv, b_send, b_recv, d_send, d_recv, t_send, t_recv,
 ):
     d = lax.axis_index("dp")
@@ -98,6 +102,14 @@
 
     lax.fori_loop(0, UNITS // 128, turn, 0)
 
+    @pl.when(f == 0)
+    def _():
+        pre[:] = jnp.zeros_like(pre)
+
+    @pl.when(f == LINE - 1)
+    def _():
+        suf[:] = jnp.zeros_like(suf)
+
     load_x.wait()
     load_mom.wait()
     load_sec.wait()
@@ -150,133 +162,156 @@
                 basis[which, 32 * x : 32 * x + 32, 128 * b : 128 * b + 128] = placed[32 * b : 32 * b + 32]
 
     def project(which):
-        half = pl.ds(pl.multiple_of(which * 128, 128), 128)
-        own[:, half] = lax.dot_general(
+        own[which] = lax.dot_general(
             x_v[...], basis[which], (((1,), (1,)), ((), ())), preferred_element_type=F32)
 
     swap_core(zh).wait()
     unfold(zh)
     project(zh)
-    each_peer(lambda i: wait_block(1 - zh, i))
-    swap_core(1 - zh).start()
-    swap_core(1 - zh).wait()
-    unfold(1 - zh)
-    project(1 - zh)
-    swap_zh.wait_send()
-    each_peer(lambda i: send_block(zh, i).wait_send())
-    each_peer(lambda i: send_block(1 - zh, i).wait_send())
-
-    @pl.when(f == 0)
-    def _():
-        pre[...] = jnp.zeros_like(pre)
-
-    @pl.when(f == LINE - 1)
-    def _():
-        suf[...] = jnp.zeros_like(suf)
-
-    def right(p):
+
+    def right(which, p):
         rows = pl.ds(pl.multiple_of(p * PIECE, PIECE), PIECE)
         return pltpu.make_async_remote_copy(
-            out_r.at[rows], pre.at[rows], r_send.at[p], r_recv.at[p],
+            out_r.at[which, rows], pre.at[which, rows], r_send.at[which, p], r_recv.at[which, p],
             device_id=(d, lax.rem(f + 1, LINE)), device_id_type=MESH)
 
-    def left(p):
+    def left(which, p):
         rows = pl.ds(pl.multiple_of(p * PIECE, PIECE), PIECE)
         return pltpu.make_async_remote_copy(
-            out_l.at[rows], suf.at[rows], l_send.at[p], l_recv.at[p],
+            out_l.at[which, rows], suf.at[which, rows], l_send.at[which, p], l_recv.at[which, p],
             device_id=(d, lax.rem(f + LINE - 1, LINE)), device_id_type=MESH)
 
+    def chain(which, t):
+        p = t - f * SKEW
+
+        @pl.when((p >= 0) & (p < PIECES))
+        def _():
+            @pl.when(f > 0)
+            def _():
+                right(which, p).wait_recv()
+
+            @pl.when(f < LINE - 1)
+            def _():
+                rows = pl.ds(pl.multiple_of(p * PIECE, PIECE), PIECE)
+                out_r[which, rows] = (own[which, rows] + pre[which, rows].astype(F32)).astype(BF16)
+                right(which, p).start()
+
+        q = t - (LINE - 1 - f) * SKEW
+
+        @pl.when((q >= 0) & (q < PIECES))
+        def _():
+            @pl.when(f < LINE - 1)
+            def _():
+                left(which, q).wait_recv()
+
+            @pl.when(f > 0)
+            def _():
+                rows = pl.ds(pl.multiple_of(q * PIECE, PIECE), PIECE)
+                out_l[which, rows] = (own[which, rows] + suf[which, rows].astype(F32)).astype(BF16)
+                left(which, q).start()
+
+    btf[448:, :] = jnp.zeros((8, 128), F32)
+
+    def swap_terms(which, x):
+        return pltpu.make_async_remote_copy(
+            btb.at[which, 1 - core, pl.ds(x * 8, 8)], cbuf.at[which, pl.ds(x * 8, 8)], t_send.at[which, x], t_recv.at[which, x],
+            device_id=other_core, device_id_type=MESH)
+
+    def make_terms(which):
+        proj[...] = (own[which] + (pre[which].astype(F32) + suf[which].astype(F32))).astype(BF16)
+
+        def terms(i, _):
+            x = lax.rem(xx + 1 + i, 4)
+            first = pl.multiple_of(x * 448, 448)
+            btf[0:448, :] = jnp.dot(got[pl.ds(first, 448), :], proj[...], preferred_element_type=F32)
+            for k in range(8):
+                two = btf[56 * k : 56 * k + 64, :]
+                j = x * 8 + (k % 4) * 2 + k // 4
+                btb[which, 0, j] = two[:PAD].astype(BF16)
+                btb[which, 1, j] = pltpu.roll(two, 64 - OWNED, 0)[:PAD].astype(BF16)
+            swap_terms(which, x).start()
+            return 0
+
+        lax.fori_loop(0, 4, terms, 0)
+
+    def send_terms(which, q):
+        return pltpu.make_async_remote_copy(
+            s1.at[which, pl.ds(q * 2, 2)], rb.at[which, pos], b_send.at[which, q], b_recv.at[which, pos],
+            device_id=at_pos(q), device_id_type=MESH)
+
+    def add_cores(which):
+        def body(i, _):
+            x = lax.rem(xx + 1 + i, 4)
+            swap_terms(which, x).wait()
+            for k in range(4):
+                q = x * 4 + lax.rem(y + 1 + k, 4)
+                both = pl.ds(q * 2, 2)
+                s1[which, both] = (btb[which, core, both].astype(F32) + cbuf[which, both].astype(F32)).astype(BF16)
+
+                @pl.when(q != pos)
+                def _():
+                    send_terms(which, q).start()
+
+            return 0
+
+        lax.fori_loop(0, 4, body, 0)
+
+    far = jnp.maximum(f, LINE - 1 - f)
+    first_done = far * SKEW + PIECES + jnp.maximum(5 - far, 0) * (LATER + 1)
+
     def step(t, _):
-        p = t - f * SKEW
-
-        @pl.when((p >= 0) & (p < PIECES))
-        def _():
-            @pl.when(f > 0)
-            def _():
-                right(p).wait_recv()
-
-            @pl.when(f < LINE - 1)
-            def _():
-                rows = pl.ds(pl.multiple_of(p * PIECE, PIECE), PIECE)
-                out_r[rows] = (own[rows] + pre[rows].astype(F32)).astype(BF16)
-                right(p).start()
-
-        q = t - (LINE - 1 - f) * SKEW
-
-        @pl.when((q >= 0) & (q < PIECES))
-        def _():
-            @pl.when(f < LINE - 1)
-            def _():
-                left(q).wait_recv()
-
-            @pl.when(f > 0)
-            def _():
-                rows = pl.ds(pl.multiple_of(q * PIECE, PIECE), PIECE)
-                out_l[rows] = (own[rows] + suf[rows].astype(F32)).astype(BF16)
-                left(q).start()
+        chain(zh, t)
+        chain(1 - zh, t - LATER)
+
+        @pl.when(t == GATHERED)
+        def _():
+            each_peer(lambda i: wait_block(1 - zh, i))
+            swap_core(1 - zh).start()
+
+        @pl.when(t == PROJECTED)
+        def _():
+            swap_core(1 - zh).wait()
+            unfold(1 - zh)
+            project(1 - zh)
+
+        @pl.when(t == first_done)
+        def _():
+            make_terms(zh)
+
+        @pl.when(t == first_done + ADDED)
+        def _():
+            add_cores(zh)
 
         return 0
 
-    lax.fori_loop(0, PIECES + (LINE - 1) * SKEW, step, 0)
-
-    proj[...] = (own[...] + (pre[...].astype(F32) + suf[...].astype(F32))).astype(BF16)
-
-    btf[448:, :] = jnp.zeros((8, RANK), F32)
-
-    def swap_terms(x):
-        return pltpu.make_async_remote_copy(
-            btb.at[1 - core, pl.ds(x * 8, 8)], cbuf.at[pl.ds(x * 8, 8)], t_send.at[x], t_recv.at[x],
-            device_id=other_core, device_id_type=MESH)
-
-    def terms(i, _):
-        x = lax.rem(xx + 1 + i, 4)
-        first = pl.multiple_of(x * 448, 448)
-        btf[0:448, :] = jnp.dot(got[pl.ds(first, 448), :], proj[...], preferred_element_type=F32)
-        for k in range(8):
-            two = btf[56 * k : 56 * k + 64, :]
-            j = x * 8 + (k % 4) * 2 + k // 4
-            btb[0, j] = two[:PAD].astype(BF16)
-            btb[1, j] = pltpu.roll(two, 64 - OWNED, 0)[:PAD].astype(BF16)
-        swap_terms(x).start()
-        return 0
-
-    lax.fori_loop(0, 4, terms, 0)
-
-    def send_terms(q):
-        return pltpu.make_async_remote_copy(
-            s1.at[pl.ds(q * 2, 2)], rb.at[pos], b_send.at[q], b_recv.at[pos], device_id=at_pos(q), device_id_type=MESH)
-
-    def add_cores(i, _):
-        x = lax.rem(xx + 1 + i, 4)
-        swap_terms(x).wait()
-        for k in range(4):
-            q = x * 4 + lax.rem(y + 1 + k, 4)
-            both = pl.ds(q * 2, 2)
-            s1[both] = (btb[core, both].astype(F32) + cbuf[both].astype(F32)).astype(BF16)
-
-            @pl.when(q != pos)
-            def _():
-                send_terms(q).start()
-
-        return 0
-
-    lax.fori_loop(0, 4, add_cores, 0)
-
-    def add_terms(i, acc):
-        q = lax.rem(pos + 16 - i, 16)
-        pltpu.make_async_remote_copy(
-            s1.at[pl.ds(q * 2, 2)], rb.at[q], b_send.at[q], b_recv.at[q],
-            device_id=at_pos(q), device_id_type=MESH).wait_recv()
-        return (acc[0] + rb[q, zh].astype(F32), acc[1] + rb[q, 1 - zh].astype(F32))
-
-    mine, theirs = lax.fori_loop(
-        1, 16, add_terms, (s1[2 * pos + zh].astype(F32), s1[2 * pos + 1 - zh].astype(F32)))
-    zsend[...] = theirs.astype(BF16)
-    swap_sum = pltpu.make_async_remote_copy(
-        zsend, zrecv, z_send.at[1], z_recv.at[1], device_id=other_zh, device_id_type=MESH)
-    swap_sum.start()
-    swap_sum.wait()
-    grad_sub = to_natural(mine + zrecv[...].astype(F32))[:OWNED]
+    lax.fori_loop(0, LATER + (LINE - 1) * SKEW + PIECES, step, 0)
+    make_terms(1 - zh)
+    add_cores(1 - zh)
+
+    def swap_sum(which):
+        return pltpu.make_async_remote_copy(
+            zsend.at[which], zrecv.at[which], z_send.at[1 + which], z_recv.at[1 + which],
+            device_id=other_zh, device_id_type=MESH)
+
+    def add_chips(which):
+        def body(i, acc):
+            q = lax.rem(pos + 16 - i, 16)
+            pltpu.make_async_remote_copy(
+                s1.at[which, pl.ds(q * 2, 2)], rb.at[which, q], b_send.at[which, q], b_recv.at[which, q],
+                device_id=at_pos(q), device_id_type=MESH).wait_recv()
+            return (acc[0] + rb[which, q, zh].astype(F32), acc[1] + rb[which, q, 1 - zh].astype(F32))
+
+        mine, theirs = lax.fori_loop(
+            1, 16, body, (s1[which, 2 * pos + zh].astype(F32), s1[which, 2 * pos + 1 - zh].astype(F32)))
+        zsend[which] = theirs.astype(BF16)
+        swap_sum(which).start()
+        total[which] = mine
+
+    add_chips(zh)
+    add_chips(1 - zh)
+    swap_sum(zh).wait()
+    swap_sum(1 - zh).wait()
+    grad_sub = to_natural(jnp.concatenate([total[h] + zrecv[h].astype(F32) for h in range(2)], axis=1))[:OWNED]
 
     moment_new, second_new, direction = adam_direction(grad_sub, mom[...], sec[...])
     mnew[...] = moment_new
@@ -308,21 +343,24 @@
     upd[...] = jnp.dot(
         dirs[...].reshape(LINE * PAD, RANK), both, preferred_element_type=F32).astype(BF16)
 
-    each_peer(lambda i: send_terms(lax.rem(pos + i, 16)).wait_send())
+    swap_zh.wait_send()
     each_line(lambda i: send_dir(i).wait_send())
-
-    def sent(p, _):
-        @pl.when(f < LINE - 1)
-        def _():
-            right(p).wait_send()
-
-        @pl.when(f > 0)
-        def _():
-            left(p).wait_send()
-
-        return 0
-
-    lax.fori_loop(0, PIECES, sent, 0)
+    for which in range(2):
+        each_peer(lambda i: send_block(which, i).wait_send())
+        each_peer(lambda i: send_terms(which, lax.rem(pos + i, 16)).wait_send())
+
+        def sent(p, _):
+            @pl.when(f < LINE - 1)
+            def _():
+                right(which, p).wait_send()
+
+            @pl.when(f > 0)
+            def _():
+                left(which, p).wait_send()
+
+            return 0
+
+        lax.fori_loop(0, PIECES, sent, 0)
 
 
 def local(inputs, grad_out, projector, moment, second):
@@ -347,29 +385,30 @@
             pltpu.VMEM((UNITS, TOKENS), BF16),
             pltpu.VMEM((2, 2, 16, 32, 128), BF16),
             pltpu.VMEM((2, 128, FEATURES), BF16),
-            pltpu.VMEM((TOKENS, RANK), F32),
-            pltpu.VMEM((TOKENS, RANK), BF16),
-            pltpu.VMEM((TOKENS, RANK), BF16),
-            pltpu.VMEM((TOKENS, RANK), BF16),
-            pltpu.VMEM((TOKENS, RANK), BF16),
-            pltpu.VMEM((TOKENS, RANK), BF16),
-            pltpu.VMEM((456, RANK), F32),
-            pltpu.VMEM((2, 32, PAD, RANK), BF16),
-            pltpu.VMEM((32, PAD, RANK), BF16),
-            pltpu.VMEM((32, PAD, RANK), BF16),
-            pltpu.VMEM((16, 2, PAD, RANK), BF16),
-            pltpu.VMEM((PAD, RANK), BF16),
-            pltpu.VMEM((PAD, RANK), BF16),
+            pltpu.VMEM((2, TOKENS, 128), F32),
+            pltpu.VMEM((2, TOKENS, 128), BF16),
+            pltpu.VMEM((2, TOKENS, 128), BF16),
+            pltpu.VMEM((2, TOKENS, 128), BF16),
+            pltpu.VMEM((2, TOKENS, 128), BF16),
+            pltpu.VMEM((TOKENS, 128), BF16),
+            pltpu.VMEM((456, 128), F32),
+            pltpu.VMEM((2, 2, 32, PAD, 128), BF16),
+            pltpu.VMEM((2, 32, PAD, 128), BF16),
+            pltpu.VMEM((2, 32, PAD, 128), BF16),
+            pltpu.VMEM((2, 16, 2, PAD, 128), BF16),
+            pltpu.VMEM((2, PAD, 128), BF16),
+            pltpu.VMEM((2, PAD, 128), BF16),
+            pltpu.VMEM((2, PAD, 128), F32),
             pltpu.VMEM((PAD, RANK), F32),
             pltpu.VMEM((LINE, PAD, RANK), BF16),
             dma((4,)),
-            dma((2,)), dma((2,)),
+            dma((3,)), dma((3,)),
             dma((2, 16)), dma((2, 16)),
             dma((2,)), dma((2,)),
-            dma((PIECES,)), dma((PIECES,)), dma((PIECES,)), dma((PIECES,)),
-            dma((16,)), dma((16,)),
+            dma((2, PIECES)), dma((2, PIECES)), dma((2, PIECES)), dma((2, PIECES)),
+            dma((2, 16)), dma((2, 16)),
             dma((LINE,)), dma((LINE,)),
-            dma((4,)), dma((4,)),
+            dma((2, 4)), dma((2, 4)),
         ],
         compiler_params=pltpu.CompilerParams(
             collective_id=0, has_side_effects=True, vmem_limit_bytes=48 * 1024 * 1024),

time: 89.5 us -> 84 us (0.939)
  Pallas kernels: 86.5 us -> 80.7 us
    pallas_call x1, Pallas kernels: 86.5 us -> 80.7 us  [local(): pl.pallas_call(kernel, out_shape=(jax.ShapeDtypeStruct((LINE * PAD, FEATU...]
where the time goes in v3:
time: 84 us; the launch traced here: 83.6 us
  Pallas kernels  80.7 us (96%)
  local copies, waits for them, and re-layouts  2.25 us (3%)
    pallas_call x1, Pallas kernels, local(): pl.pallas_call(kernel, out_shape=(jax.ShapeDtypeStruct((LINE * PAD, FEATU...  80.7 us
    unnamed x3, local copies, waits for them, and re-layouts  2.25 us

profile of v3, /device:TPU:24, one launch (start us, length us, event | category | flops | bytes accessed | tf_op | source)
XLA Modules:
  0.0 83.6 jit_solution(10000770914799326671)
XLA Ops:
  0.6 80.7 %shard_map.76 = (bf16[256,1024]{1,0:T(8,128)(2,1)S(1)}, f32[28,256]{1,0:T(8,128)S(1)}, f32[28,256]{1,0:T(8,128)S(1)}) custom-call(bf16[32,128]{1,0:T(8,128)(2,1)} %bitcast.10, bf16[768,1024]{1,0:T(8,128)(2,1)} %x_hbm.1, bf16[768,1792]{1,0:T(8,128)(2,1)} %go_hbm.1, f32[28,256]{1,0:T(8,128)} %mom_hbm.1, f32[28,256]{1,0:T(8,128)} %sec_hbm.1), custom_call_target="tpu_custom_call" | custom-call | tf_op jit(solution)/shard_map/pallas_call | solution.py:371
  81.4 1.0 %copy.10 = bf16[8,28,1024]{2,0,1:T(8,128)(2,1)} copy(bf16[8,28,1024]{2,1,0:T(8,128)(2,1)S(1)} %bitcast.9) | data formatting | bytes 917504
  82.4 0.6 copy.13
  83.0 0.6 copy.14

commit v4 on v3

--- a/solution.py
+++ b/solution.py
@@ -23,13 +23,16 @@
 OWNED = 28
 PAD = 32
 LINE = 8
+PAIRS = LINE // 2
+SHARE = TOKENS // 2
 PIECE = 64
-PIECES = TOKENS // PIECE
-SKEW = 9
-GATHERED = 12
-PROJECTED = 17
-LATER = 24
-ADDED = 5
+PIECES = SHARE // PIECE
+MERGED = 5
+SKEW = 6
+GATHERED = 8
+PROJECTED = 11
+LATER = 15
+ADDED = 4
 
 
 def adam_direction(grad_sub, moment, second):
@@ -52,8 +55,9 @@
 def kernel(
     blk, x_hbm, go_hbm, mom_hbm, sec_hbm,
     upd, mnew, snew,
-    x_v, go_v, mom, sec, got, raw, basis, own, pre, suf, out_r, out_l, proj, btf, btb, cbuf, s1, rb, zsend, zrecv, total, direct, dirs,
+    x_v, go_v, mom, sec, got, raw, basis, own, out_p, pair_in, pre, suf, out_r, out_l, proj, btf, btb, cbuf, s1, rb, zsend, zrecv, total, direct, dirs,
     load_sem, z_send, z_recv, g_send, g_recv, c_send, c_recv, r_send, r_recv, l_send, l_recv, b_send, b_recv, d_send, d_recv, t_send, t_recv,
+    p_send, p_recv, q_send, q_recv,
 ):
     d = lax.axis_index("dp")
     f = lax.axis_index("fsdp")
@@ -62,6 +66,9 @@
     zh = lax.rem(d // 8, 2)
     xx = d // 16
     pos = xx * 4 + y
+    pair = f // 2
+    side = lax.rem(f, 2)
+    other_side = (d, f + 1 - 2 * side)
     other_core = (d + 1 - 2 * core, f)
     other_zh = (d + 8 - 16 * zh, f)
 
@@ -102,11 +109,11 @@
 
     lax.fori_loop(0, UNITS // 128, turn, 0)
 
-    @pl.when(f == 0)
+    @pl.when(pair == 0)
     def _():
         pre[:] = jnp.zeros_like(pre)
 
-    @pl.when(f == LINE - 1)
+    @pl.when(pair == PAIRS - 1)
     def _():
         suf[:] = jnp.zeros_like(suf)
 
@@ -169,95 +176,147 @@
     unfold(zh)
     project(zh)
 
+    def mine_at(p):
+        return pl.ds(pl.multiple_of(side * SHARE + p * PIECE, PIECE), PIECE)
+
+    def give(which, p):
+        rows = pl.ds(pl.multiple_of(p * PIECE, PIECE), PIECE)
+        return pltpu.make_async_remote_copy(
+            out_p.at[which, rows], pair_in.at[which, rows], p_send.at[which, p], p_recv.at[which, p],
+            device_id=other_side, device_id_type=MESH)
+
     def right(which, p):
         rows = pl.ds(pl.multiple_of(p * PIECE, PIECE), PIECE)
         return pltpu.make_async_remote_copy(
             out_r.at[which, rows], pre.at[which, rows], r_send.at[which, p], r_recv.at[which, p],
-            device_id=(d, lax.rem(f + 1, LINE)), device_id_type=MESH)
+            device_id=(d, lax.rem(f + 2, LINE)), device_id_type=MESH)
 
     def left(which, p):
         rows = pl.ds(pl.multiple_of(p * PIECE, PIECE), PIECE)
         return pltpu.make_async_remote_copy(
             out_l.at[which, rows], suf.at[which, rows], l_send.at[which, p], l_recv.at[which, p],
-            device_id=(d, lax.rem(f + LINE - 1, LINE)), device_id_type=MESH)
+            device_id=(d, lax.rem(f + LINE - 2, LINE)), device_id_type=MESH)
+
+    def share(which, p):
+        rows = mine_at(p)
+        return pltpu.make_async_remote_copy(
+            proj.at[which, rows], proj.at[which, rows], q_send.at[which, p], q_recv.at[which, p],
+            device_id=other_side, device_id_type=MESH)
+
+    def shared(which, p):
+        rows = pl.ds(pl.multiple_of((1 - side) * SHARE + p * PIECE, PIECE), PIECE)
+        return pltpu.make_async_remote_copy(
+            proj.at[which, rows], proj.at[which, rows], q_send.at[which, p], q_recv.at[which, p],
+            device_id=other_side, device_id_type=MESH)
+
+    far = jnp.maximum(pair, PAIRS - 1 - pair)
 
     def chain(which, t):
-        p = t - f * SKEW
+        @pl.when((t >= 0) & (t < PIECES))
+        def _():
+            rows = pl.ds(pl.multiple_of(t * PIECE, PIECE), PIECE)
+            theirs = pl.ds(pl.multiple_of((1 - side) * SHARE + t * PIECE, PIECE), PIECE)
+            out_p[which, rows] = own[which, theirs].astype(BF16)
+            give(which, t).start()
+
+        m = t - MERGED
+
+        @pl.when((m >= 0) & (m < PIECES))
+        def _():
+            give(which, m).wait_recv()
+            rows = pl.ds(pl.multiple_of(m * PIECE, PIECE), PIECE)
+            own[which, mine_at(m)] += pair_in[which, rows].astype(F32)
+
+        p = m - pair * SKEW
 
         @pl.when((p >= 0) & (p < PIECES))
         def _():
-            @pl.when(f > 0)
+            @pl.when(pair > 0)
             def _():
                 right(which, p).wait_recv()
 
-            @pl.when(f < LINE - 1)
+            @pl.when(pair < PAIRS - 1)
             def _():
                 rows = pl.ds(pl.multiple_of(p * PIECE, PIECE), PIECE)
-                out_r[which, rows] = (own[which, rows] + pre[which, rows].astype(F32)).astype(BF16)
+                out_r[which, rows] = (own[which, mine_at(p)] + pre[which, rows].astype(F32)).astype(BF16)
                 right(which, p).start()
 
-        q = t - (LINE - 1 - f) * SKEW
+        q = m - (PAIRS - 1 - pair) * SKEW
 
         @pl.when((q >= 0) & (q < PIECES))
         def _():
-            @pl.when(f < LINE - 1)
+            @pl.when(pair < PAIRS - 1)
             def _():
                 left(which, q).wait_recv()
 
-            @pl.when(f > 0)
+            @pl.when(pair > 0)
             def _():
                 rows = pl.ds(pl.multiple_of(q * PIECE, PIECE), PIECE)
-                out_l[which, rows] = (own[which, rows] + suf[which, rows].astype(F32)).astype(BF16)
+                out_l[which, rows] = (own[which, mine_at(q)] + suf[which, rows].astype(F32)).astype(BF16)
                 left(which, q).start()
 
-    btf[448:, :] = jnp.zeros((8, 128), F32)
-
-    def swap_terms(which, x):
-        return pltpu.make_async_remote_copy(
-            btb.at[which, 1 - core, pl.ds(x * 8, 8)], cbuf.at[which, pl.ds(x * 8, 8)], t_send.at[which, x], t_recv.at[which, x],
+        e = m - far * SKEW
+
+        @pl.when((e >= 0) & (e < PIECES))
+        def _():
+            rows = pl.ds(pl.multiple_of(e * PIECE, PIECE), PIECE)
+            proj[which, mine_at(e)] = (
+                own[which, mine_at(e)] + (pre[which, rows].astype(F32) + suf[which, rows].astype(F32))).astype(BF16)
+            share(which, e).start()
+
+    btf[224:, :] = jnp.zeros((8, 128), F32)
+
+    def swap_terms(which, z, x):
+        rows = pl.ds(x * 4, 4)
+        return pltpu.make_async_remote_copy(
+            btb.at[which, 1 - core, z, rows], cbuf.at[which, z, rows], t_send.at[which, z, x], t_recv.at[which, z, x],
             device_id=other_core, device_id_type=MESH)
 
+    def turn_of(i):
+        return (lax.rem(1 - zh + i // 4, 2), lax.rem(xx + 1 + i, 4))
+
     def make_terms(which):
-        proj[...] = (own[which] + (pre[which].astype(F32) + suf[which].astype(F32))).astype(BF16)
+        def arrived(p, _):
+            shared(which, p).wait_recv()
+            return 0
+
+        lax.fori_loop(0, PIECES, arrived, 0)
 
         def terms(i, _):
-            x = lax.rem(xx + 1 + i, 4)
-            first = pl.multiple_of(x * 448, 448)
-            btf[0:448, :] = jnp.dot(got[pl.ds(first, 448), :], proj[...], preferred_element_type=F32)
-            for k in range(8):
+            z, x = turn_of(i)
+            first = pl.multiple_of(x * 448 + z * 224, 32)
+            btf[0:224, :] = jnp.dot(got[pl.ds(first, 224), :], proj[which], preferred_element_type=F32)
+            for k in range(4):
                 two = btf[56 * k : 56 * k + 64, :]
-                j = x * 8 + (k % 4) * 2 + k // 4
-                btb[which, 0, j] = two[:PAD].astype(BF16)
-                btb[which, 1, j] = pltpu.roll(two, 64 - OWNED, 0)[:PAD].astype(BF16)
-            swap_terms(which, x).start()
+                btb[which, 0, z, x * 4 + k] = two[:PAD].astype(BF16)
+                btb[which, 1, z, x * 4 + k] = pltpu.roll(two, 64 - OWNED, 0)[:PAD].astype(BF16)
+            swap_terms(which, z, x).start()
             return 0
 
-        lax.fori_loop(0, 4, terms, 0)
-
-    def send_terms(which, q):
-        return pltpu.make_async_remote_copy(
-            s1.at[which, pl.ds(q * 2, 2)], rb.at[which, pos], b_send.at[which, q], b_recv.at[which, pos],
+        lax.fori_loop(0, 8, terms, 0)
+
+    def send_terms(which, z, q):
+        return pltpu.make_async_remote_copy(
+            s1.at[which, z, q], rb.at[which, z, pos], b_send.at[which, z, q], b_recv.at[which, z, pos],
             device_id=at_pos(q), device_id_type=MESH)
 
     def add_cores(which):
         def body(i, _):
-            x = lax.rem(xx + 1 + i, 4)
-            swap_terms(which, x).wait()
+            z, x = turn_of(i)
+            swap_terms(which, z, x).wait()
             for k in range(4):
                 q = x * 4 + lax.rem(y + 1 + k, 4)
-                both = pl.ds(q * 2, 2)
-                s1[which, both] = (btb[which, core, both].astype(F32) + cbuf[which, both].astype(F32)).astype(BF16)
+                s1[which, z, q] = (btb[which, core, z, q].astype(F32) + cbuf[which, z, q].astype(F32)).astype(BF16)
 
                 @pl.when(q != pos)
                 def _():
-                    send_terms(which, q).start()
+                    send_terms(which, z, q).start()
 
             return 0
 
-        lax.fori_loop(0, 4, body, 0)
-
-    far = jnp.maximum(f, LINE - 1 - f)
-    first_done = far * SKEW + PIECES + jnp.maximum(5 - far, 0) * (LATER + 1)
+        lax.fori_loop(0, 8, body, 0)
+
+    first_done = MERGED + far * SKEW + PIECES + (far - 2) * MERGED + (3 - far) * (LATER + 1)
 
     def step(t, _):
         chain(zh, t)
@@ -284,7 +343,7 @@
 
         return 0
 
-    lax.fori_loop(0, LATER + (LINE - 1) * SKEW + PIECES, step, 0)
+    lax.fori_loop(0, LATER + MERGED + (PAIRS - 1) * SKEW + PIECES + ADDED, step, 0)
     make_terms(1 - zh)
     add_cores(1 - zh)
 
@@ -293,22 +352,23 @@
             zsend.at[which], zrecv.at[which], z_send.at[1 + which], z_recv.at[1 + which],
             device_id=other_zh, device_id_type=MESH)
 
-    def add_chips(which):
+    def add_chips(which, z):
         def body(i, acc):
             q = lax.rem(pos + 16 - i, 16)
             pltpu.make_async_remote_copy(
-                s1.at[which, pl.ds(q * 2, 2)], rb.at[which, q], b_send.at[which, q], b_recv.at[which, q],
+                s1.at[which, z, q], rb.at[which, z, q], b_send.at[which, z, q], b_recv.at[which, z, q],
                 device_id=at_pos(q), device_id_type=MESH).wait_recv()
-            return (acc[0] + rb[which, q, zh].astype(F32), acc[1] + rb[which, q, 1 - zh].astype(F32))
-
-        mine, theirs = lax.fori_loop(
-            1, 16, body, (s1[which, 2 * pos + zh].astype(F32), s1[which, 2 * pos + 1 - zh].astype(F32)))
-        zsend[which] = theirs.astype(BF16)
+            return acc + rb[which, z, q].astype(F32)
+
+        return lax.fori_loop(1, 16, body, s1[which, z, pos].astype(F32))
+
+    for which in (zh, 1 - zh):
+        zsend[which] = add_chips(which, 1 - zh).astype(BF16)
         swap_sum(which).start()
-        total[which] = mine
-
-    add_chips(zh)
-    add_chips(1 - zh)
+
+    for which in (zh, 1 - zh):
+        total[which] = add_chips(which, zh)
+
     swap_sum(zh).wait()
     swap_sum(1 - zh).wait()
     grad_sub = to_natural(jnp.concatenate([total[h] + zrecv[h].astype(F32) for h in range(2)], axis=1))[:OWNED]
@@ -340,21 +400,28 @@
 
     each_line(wait_dir)
     both = basis[...].reshape(RANK, FEATURES)
-    upd[...] = jnp.dot(
-        dirs[...].reshape(LINE * PAD, RANK), both, preferred_element_type=F32).astype(BF16)
+    row = lax.broadcasted_iota(jnp.int32, (OWNED * LINE, LINE * PAD), 0)
+    col = lax.broadcasted_iota(jnp.int32, (OWNED * LINE, LINE * PAD), 1)
+    order = jnp.where(col == (row % LINE) * PAD + row // LINE, 1.0, 0.0).astype(BF16)
+    ordered = jnp.dot(order, dirs[...].reshape(LINE * PAD, RANK), preferred_element_type=F32).astype(BF16)
+    upd[...] = jnp.dot(ordered, both, preferred_element_type=F32).astype(BF16)
 
     swap_zh.wait_send()
     each_line(lambda i: send_dir(i).wait_send())
     for which in range(2):
         each_peer(lambda i: send_block(which, i).wait_send())
-        each_peer(lambda i: send_terms(which, lax.rem(pos + i, 16)).wait_send())
+        for z in range(2):
+            each_peer(lambda i: send_terms(which, z, lax.rem(pos + i, 16)).wait_send())
 
         def sent(p, _):
-            @pl.when(f < LINE - 1)
+            give(which, p).wait_send()
+            share(which, p).wait_send()
+
+            @pl.when(pair < PAIRS - 1)
             def _():
                 right(which, p).wait_send()
 
-            @pl.when(f > 0)
+            @pl.when(pair > 0)
             def _():
                 left(which, p).wait_send()
 
@@ -371,7 +438,7 @@
     update, moment_new, second_new = pl.pallas_call(
         kernel,
         out_shape=(
-            jax.ShapeDtypeStruct((LINE * PAD, FEATURES), BF16),
+            jax.ShapeDtypeStruct((OWNED * LINE, FEATURES), BF16),
             jax.ShapeDtypeStruct((OWNED, RANK), F32),
             jax.ShapeDtypeStruct((OWNED, RANK), F32),
         ),
@@ -386,16 +453,18 @@
             pltpu.VMEM((2, 2, 16, 32, 128), BF16),
             pltpu.VMEM((2, 128, FEATURES), BF16),
             pltpu.VMEM((2, TOKENS, 128), F32),
+            pltpu.VMEM((2, SHARE, 128), BF16),
+            pltpu.VMEM((2, SHARE, 128), BF16),
+            pltpu.VMEM((2, SHARE, 128), BF16),
+            pltpu.VMEM((2, SHARE, 128), BF16),
+            pltpu.VMEM((2, SHARE, 128), BF16),
+            pltpu.VMEM((2, SHARE, 128), BF16),
             pltpu.VMEM((2, TOKENS, 128), BF16),
-            pltpu.VMEM((2, TOKENS, 128), BF16),
-            pltpu.VMEM((2, TOKENS, 128), BF16),
-            pltpu.VMEM((2, TOKENS, 128), BF16),
-            pltpu.VMEM((TOKENS, 128), BF16),
-            pltpu.VMEM((456, 128), F32),
-            pltpu.VMEM((2, 2, 32, PAD, 128), BF16),
-            pltpu.VMEM((2, 32, PAD, 128), BF16),
-            pltpu.VMEM((2, 32, PAD, 128), BF16),
-            pltpu.VMEM((2, 16, 2, PAD, 128), BF16),
+            pltpu.VMEM((232, 128), F32),
+            pltpu.VMEM((2, 2, 2, 16, PAD, 128), BF16),
+            pltpu.VMEM((2, 2, 16, PAD, 128), BF16),
+            pltpu.VMEM((2, 2, 16, PAD, 128), BF16),
+            pltpu.VMEM((2, 2, 16, PAD, 128), BF16),
             pltpu.VMEM((2, PAD, 128), BF16),
             pltpu.VMEM((2, PAD, 128), BF16),
             pltpu.VMEM((2, PAD, 128), F32),
@@ -406,14 +475,15 @@
             dma((2, 16)), dma((2, 16)),
             dma((2,)), dma((2,)),
             dma((2, PIECES)), dma((2, PIECES)), dma((2, PIECES)), dma((2, PIECES)),
-            dma((2, 16)), dma((2, 16)),
+            dma((2, 2, 16)), dma((2, 2, 16)),
             dma((LINE,)), dma((LINE,)),
-            dma((2, 4)), dma((2, 4)),
+            dma((2, 2, 4)), dma((2, 2, 4)),
+            dma((2, PIECES)), dma((2, PIECES)), dma((2, PIECES)), dma((2, PIECES)),
         ],
         compiler_params=pltpu.CompilerParams(
             collective_id=0, has_side_effects=True, vmem_limit_bytes=48 * 1024 * 1024),
     )(*[pltpu.with_memory_space_constraint(v, pltpu.HBM) for v in (blk, inputs, grad_out, moment, second)])
-    return (update.reshape(LINE, PAD, FEATURES)[:, :OWNED], moment_new, second_new)
+    return (update.reshape(OWNED, LINE, FEATURES).transpose(1, 0, 2), moment_new, second_new)
 
 
 def solution(mesh):

time: 84 us -> 82 us (0.976)
  Pallas kernels: 80.7 us -> 78.2 us
    pallas_call x1, Pallas kernels: 80.7 us -> 78.2 us  [local(): pl.pallas_call(kernel, out_shape=(jax.ShapeDtypeStruct((OWNED * LINE, FEA...]
where the time goes in v4:
time: 82 us; the launch traced here: 80.8 us
  Pallas kernels  78.2 us (95%)
  local copies, waits for them, and re-layouts  2 us (2%)
    pallas_call x1, Pallas kernels, local(): pl.pallas_call(kernel, out_shape=(jax.ShapeDtypeStruct((OWNED * LINE, FEA...  78.2 us
    unnamed x3, local copies, waits for them, and re-layouts  2 us

profile of v4, /device:TPU:24, one launch (start us, length us, event | category | flops | bytes accessed | tf_op | source)
XLA Modules:
  0.0 80.8 jit_solution(2094453916684615945)
XLA Ops:
  0.6 78.2 %shard_map.76 = (bf16[224,1024]{1,0:T(8,128)(2,1)S(1)}, f32[28,256]{1,0:T(8,128)S(1)}, f32[28,256]{1,0:T(8,128)S(1)}) custom-call(bf16[32,128]{1,0:T(8,128)(2,1)} %bitcast.11, bf16[768,1024]{1,0:T(8,128)(2,1)} %x_hbm.1, bf16[768,1792]{1,0:T(8,128)(2,1)} %go_hbm.1, f32[28,256]{1,0:T(8,128)} %mom_hbm.1, f32[28,256]{1,0:T(8,128)} %sec_hbm.1), custom_call_target="tpu_custom_call" | custom-call | tf_op jit(solution)/shard_map/pallas_call | solution.py:438
  78.8 0.8 copy.12
  79.6 0.6 copy.13
  80.2 0.6 copy.14

commit v5 on v4

--- a/solution.py
+++ b/solution.py
@@ -25,14 +25,15 @@
 LINE = 8
 PAIRS = LINE // 2
 SHARE = TOKENS // 2
-PIECE = 64
+PIECE = 128
 PIECES = SHARE // PIECE
-MERGED = 5
-SKEW = 6
-GATHERED = 8
-PROJECTED = 11
-LATER = 15
+MERGED = 3
+SKEW = 4
+GATHERED = 4
+PROJECTED = 5
+LATER = 7
 ADDED = 4
+BEHIND = 3
 
 
 def adam_direction(grad_sub, moment, second):
@@ -53,7 +54,7 @@
 
 
 def kernel(
-    blk, x_hbm, go_hbm, mom_hbm, sec_hbm,
+    blk_hbm, x_hbm, go_hbm, mom_hbm, sec_hbm,
     upd, mnew, snew,
     x_v, go_v, mom, sec, got, raw, basis, own, out_p, pair_in, pre, suf, out_r, out_l, proj, btf, btb, cbuf, s1, rb, zsend, zrecv, total, direct, dirs,
     load_sem, z_send, z_recv, g_send, g_recv, c_send, c_recv, r_send, r_recv, l_send, l_recv, b_send, b_recv, d_send, d_recv, t_send, t_recv,
@@ -75,40 +76,32 @@
     def at_pos(q):
         return (((q // 4) * 2 + zh) * 8 + lax.rem(q, 4) * 2 + core, f)
 
+    barrier = pltpu.get_barrier_semaphore()
+    pl.semaphore_signal(barrier, inc=1, device_id=other_zh, device_id_type=MESH)
+    pl.semaphore_signal(barrier, inc=1, device_id=other_core, device_id_type=MESH)
+
+    def greet_line(i, _):
+        pl.semaphore_signal(barrier, inc=1, device_id=(d, lax.rem(f + i, LINE)), device_id_type=MESH)
+        return 0
+
+    lax.fori_loop(1, LINE, greet_line, 0)
+
+    def greet(i, _):
+        pl.semaphore_signal(barrier, inc=1, device_id=at_pos(lax.rem(pos + i, 16)), device_id_type=MESH)
+        return 0
+
+    lax.fori_loop(1, 16, greet, 0)
+
     load_x = pltpu.make_async_copy(x_hbm, x_v, load_sem.at[0])
     load_go = pltpu.make_async_copy(go_hbm, go_v, load_sem.at[1])
     load_mom = pltpu.make_async_copy(mom_hbm, mom, load_sem.at[2])
     load_sec = pltpu.make_async_copy(sec_hbm, sec, load_sem.at[3])
+    load_blk = pltpu.make_async_copy(blk_hbm, raw.at[zh, core, pos], load_sem.at[4])
+    load_blk.start()
     load_go.start()
     load_x.start()
     load_mom.start()
     load_sec.start()
-
-    barrier = pltpu.get_barrier_semaphore()
-    pl.semaphore_signal(barrier, inc=1, device_id=other_zh, device_id_type=MESH)
-    pl.semaphore_signal(barrier, inc=1, device_id=other_core, device_id_type=MESH)
-
-    def greet(i, _):
-        pl.semaphore_signal(barrier, inc=1, device_id=at_pos(lax.rem(pos + i, 16)), device_id_type=MESH)
-        return 0
-
-    lax.fori_loop(1, 16, greet, 0)
-
-    def greet_line(i, _):
-        pl.semaphore_signal(barrier, inc=1, device_id=(d, lax.rem(f + i, LINE)), device_id_type=MESH)
-        return 0
-
-    lax.fori_loop(1, LINE, greet_line, 0)
-    raw[zh, core, pos] = blk[...]
-    load_go.wait()
-
-    def turn(i, _):
-        cols = pl.ds(pl.multiple_of(i * 128, 128), 128)
-        got[cols, :] = go_v[:, cols].T
-        return 0
-
-    lax.fori_loop(0, UNITS // 128, turn, 0)
-
     @pl.when(pair == 0)
     def _():
         pre[:] = jnp.zeros_like(pre)
@@ -120,6 +113,8 @@
     load_x.wait()
     load_mom.wait()
     load_sec.wait()
+    load_go.wait()
+    load_blk.wait()
     pl.semaphore_wait(barrier, 24)
 
     def send_block(which, i):
@@ -149,6 +144,13 @@
         return pltpu.make_async_remote_copy(
             raw.at[which, core], raw.at[which, core], c_send.at[which], c_recv.at[which],
             device_id=other_core, device_id_type=MESH)
+
+    def turn(i, _):
+        cols = pl.ds(pl.multiple_of(i * 128, 128), 128)
+        got[cols, :] = go_v[:, cols].T
+        return 0
+
+    lax.fori_loop(0, UNITS // 128, turn, 0)
 
     each_peer(lambda i: wait_block(zh, i))
     swap_core(zh).start()
@@ -275,13 +277,14 @@
     def turn_of(i):
         return (lax.rem(1 - zh + i // 4, 2), lax.rem(xx + 1 + i, 4))
 
-    def make_terms(which):
+    def all_shared(which):
         def arrived(p, _):
             shared(which, p).wait_recv()
             return 0
 
         lax.fori_loop(0, PIECES, arrived, 0)
 
+    def terms_of(which):
         def terms(i, _):
             z, x = turn_of(i)
             first = pl.multiple_of(x * 448 + z * 224, 32)
@@ -293,15 +296,55 @@
             swap_terms(which, z, x).start()
             return 0
 
-        lax.fori_loop(0, 8, terms, 0)
+        return terms
+
+    def make_terms(which):
+        all_shared(which)
+        lax.fori_loop(0, 8, terms_of(which), 0)
 
     def send_terms(which, z, q):
         return pltpu.make_async_remote_copy(
             s1.at[which, z, q], rb.at[which, z, pos], b_send.at[which, z, q], b_recv.at[which, z, pos],
             device_id=at_pos(q), device_id_type=MESH)
 
-    def add_cores(which):
+    def send_both(which, q):
+        return pltpu.make_async_remote_copy(
+            s1.at[which, pl.ds(0, 2), q], rb.at[which, pl.ds(0, 2), pos], b_send.at[which, 0, q], b_recv.at[which, 0, pos],
+            device_id=at_pos(q), device_id_type=MESH)
+
+    def add_cores_first(which):
         def body(i, _):
+            x = lax.rem(xx + 1 + i, 4)
+            for z in range(2):
+                swap_terms(which, z, x).wait()
+            for k in range(4):
+                q = x * 4 + lax.rem(y + 1 + k, 4)
+                for z in range(2):
+                    s1[which, z, q] = (btb[which, core, z, q].astype(F32) + cbuf[which, z, q].astype(F32)).astype(BF16)
+
+                @pl.when(q != pos)
+                def _():
+                    send_both(which, q).start()
+
+            return 0
+
+        lax.fori_loop(0, 4, body, 0)
+
+    def make_and_add(which):
+        terms = terms_of(which)
+
+        def body(step, _):
+            @pl.when(step < 8)
+            def _():
+                terms(step, 0)
+
+            @pl.when(step >= BEHIND)
+            def _():
+                add(step - BEHIND)
+
+            return 0
+
+        def add(i):
             z, x = turn_of(i)
             swap_terms(which, z, x).wait()
             for k in range(4):
@@ -312,9 +355,8 @@
                 def _():
                     send_terms(which, z, q).start()
 
-            return 0
-
-        lax.fori_loop(0, 8, body, 0)
+        all_shared(which)
+        lax.fori_loop(0, 8 + BEHIND, body, 0)
 
     first_done = MERGED + far * SKEW + PIECES + (far - 2) * MERGED + (3 - far) * (LATER + 1)
 
@@ -339,13 +381,12 @@
 
         @pl.when(t == first_done + ADDED)
         def _():
-            add_cores(zh)
+            add_cores_first(zh)
 
         return 0
 
     lax.fori_loop(0, LATER + MERGED + (PAIRS - 1) * SKEW + PIECES + ADDED, step, 0)
-    make_terms(1 - zh)
-    add_cores(1 - zh)
+    make_and_add(1 - zh)
 
     def swap_sum(which):
         return pltpu.make_async_remote_copy(
@@ -362,13 +403,23 @@
 
         return lax.fori_loop(1, 16, body, s1[which, z, pos].astype(F32))
 
-    for which in (zh, 1 - zh):
-        zsend[which] = add_chips(which, 1 - zh).astype(BF16)
-        swap_sum(which).start()
-
-    for which in (zh, 1 - zh):
-        total[which] = add_chips(which, zh)
-
+    def add_chips_first(which):
+        def body(i, acc):
+            q = lax.rem(pos + 16 - i, 16)
+            pltpu.make_async_remote_copy(
+                s1.at[which, pl.ds(0, 2), q], rb.at[which, pl.ds(0, 2), q], b_send.at[which, 0, q], b_recv.at[which, 0, q],
+                device_id=at_pos(q), device_id_type=MESH).wait_recv()
+            return (acc[0] + rb[which, zh, q].astype(F32), acc[1] + rb[which, 1 - zh, q].astype(F32))
+
+        return lax.fori_loop(1, 16, body, (s1[which, zh, pos].astype(F32), s1[which, 1 - zh, pos].astype(F32)))
+
+    mine, theirs = add_chips_first(zh)
+    total[zh] = mine
+    zsend[zh] = theirs.astype(BF16)
+    swap_sum(zh).start()
+    zsend[1 - zh] = add_chips(1 - zh, 1 - zh).astype(BF16)
+    swap_sum(1 - zh).start()
+    total[1 - zh] = add_chips(1 - zh, zh)
     swap_sum(zh).wait()
     swap_sum(1 - zh).wait()
     grad_sub = to_natural(jnp.concatenate([total[h] + zrecv[h].astype(F32) for h in range(2)], axis=1))[:OWNED]
@@ -408,10 +459,11 @@
 
     swap_zh.wait_send()
     each_line(lambda i: send_dir(i).wait_send())
+    each_peer(lambda i: send_both(zh, lax.rem(pos + i, 16)).wait_send())
+    for z in range(2):
+        each_peer(lambda i: send_terms(1 - zh, z, lax.rem(pos + i, 16)).wait_send())
     for which in range(2):
         each_peer(lambda i: send_block(which, i).wait_send())
-        for z in range(2):
-            each_peer(lambda i: send_terms(which, z, lax.rem(pos + i, 16)).wait_send())
 
         def sent(p, _):
             give(which, p).wait_send()
@@ -442,7 +494,7 @@
             jax.ShapeDtypeStruct((OWNED, RANK), F32),
             jax.ShapeDtypeStruct((OWNED, RANK), F32),
         ),
-        in_specs=[vmem, anywhere, anywhere, anywhere, anywhere],
+        in_specs=[anywhere, anywhere, anywhere, anywhere, anywhere],
         out_specs=(vmem, vmem, vmem),
         scratch_shapes=[
             pltpu.VMEM((TOKENS, FEATURES), BF16),
@@ -470,7 +522,7 @@
             pltpu.VMEM((2, PAD, 128), F32),
             pltpu.VMEM((PAD, RANK), F32),
             pltpu.VMEM((LINE, PAD, RANK), BF16),
-            dma((4,)),
+            dma((5,)),
             dma((3,)), dma((3,)),
             dma((2, 16)), dma((2, 16)),
             dma((2,)), dma((2,)),

time: 82 us -> 79.7 us (0.972)
  Pallas kernels: 78.2 us -> 75.7 us
    pallas_call x1, Pallas kernels: 78.2 us -> 75.7 us  [local(): pl.pallas_call(kernel, out_shape=(jax.ShapeDtypeStruct((OWNED * LINE, FEA...]
where the time goes in v5:
time: 79.7 us; the launch traced here: 78.4 us
  Pallas kernels  75.7 us (95%)
  local copies, waits for them, and re-layouts  2 us (3%)
    pallas_call x1, Pallas kernels, local(): pl.pallas_call(kernel, out_shape=(jax.ShapeDtypeStruct((OWNED * LINE, FEA...  75.7 us
    unnamed x3, local copies, waits for them, and re-layouts  2 us

profile of v5, /device:TPU:24, one launch (start us, length us, event | category | flops | bytes accessed | tf_op | source)
XLA Modules:
  0.0 78.4 jit_solution(6587380867699875587)
XLA Ops:
  0.6 75.7 %shard_map.76 = (bf16[224,1024]{1,0:T(8,128)(2,1)S(1)}, f32[28,256]{1,0:T(8,128)S(1)}, f32[28,256]{1,0:T(8,128)S(1)}) custom-call(bf16[32,128]{1,0:T(8,128)(2,1)} %bitcast.11, bf16[768,1024]{1,0:T(8,128)(2,1)} %x_hbm.1, bf16[768,1792]{1,0:T(8,128)(2,1)} %go_hbm.1, f32[28,256]{1,0:T(8,128)} %mom_hbm.1, f32[28,256]{1,0:T(8,128)} %sec_hbm.1), custom_call_target="tpu_custom_call" | custom-call | tf_op jit(solution)/shard_map/pallas_call | solution.py:490
  76.4 0.8 copy.12
  77.2 0.6 copy.13
  77.8 0.6 copy.14

commit v6 on v5

--- a/solution.py
+++ b/solution.py
@@ -55,8 +55,8 @@
 
 def kernel(
     blk_hbm, x_hbm, go_hbm, mom_hbm, sec_hbm,
-    upd, mnew, snew,
-    x_v, go_v, mom, sec, got, raw, basis, own, out_p, pair_in, pre, suf, out_r, out_l, proj, btf, btb, cbuf, s1, rb, zsend, zrecv, total, direct, dirs,
+    upd, grad,
+    x_v, go_v, mom, sec, got, raw, basis, own, out_p, pair_in, pre, suf, out_r, out_l, proj, early, btf, btb, cbuf, s1, rb, zsend, zrecv, total, direct, dirs,
     load_sem, z_send, z_recv, g_send, g_recv, c_send, c_recv, r_send, r_recv, l_send, l_recv, b_send, b_recv, d_send, d_recv, t_send, t_recv,
     p_send, p_recv, q_send, q_recv,
 ):
@@ -102,18 +102,7 @@
     load_x.start()
     load_mom.start()
     load_sec.start()
-    @pl.when(pair == 0)
-    def _():
-        pre[:] = jnp.zeros_like(pre)
-
-    @pl.when(pair == PAIRS - 1)
-    def _():
-        suf[:] = jnp.zeros_like(suf)
-
-    load_x.wait()
-    load_mom.wait()
-    load_sec.wait()
-    load_go.wait()
+
     load_blk.wait()
     pl.semaphore_wait(barrier, 24)
 
@@ -150,7 +139,16 @@
         got[cols, :] = go_v[:, cols].T
         return 0
 
+    load_go.wait()
     lax.fori_loop(0, UNITS // 128, turn, 0)
+
+    @pl.when(pair == 0)
+    def _():
+        pre[:] = jnp.zeros_like(pre)
+
+    @pl.when(pair == PAIRS - 1)
+    def _():
+        suf[:] = jnp.zeros_like(suf)
 
     each_peer(lambda i: wait_block(zh, i))
     swap_core(zh).start()
@@ -174,6 +172,9 @@
         own[which] = lax.dot_general(
             x_v[...], basis[which], (((1,), (1,)), ((), ())), preferred_element_type=F32)
 
+    load_x.wait()
+    load_mom.wait()
+    load_sec.wait()
     swap_core(zh).wait()
     unfold(zh)
     project(zh)
@@ -284,11 +285,23 @@
 
         lax.fori_loop(0, PIECES, arrived, 0)
 
+    mine_half = pl.ds(pl.multiple_of(side * SHARE, 128), SHARE)
+    their_half = pl.ds(pl.multiple_of((1 - side) * SHARE, 128), SHARE)
+
+    def early_terms(which):
+        def body(i, _):
+            rows = pl.ds(pl.multiple_of(i * 448, 32), 448)
+            early[rows, :] = jnp.dot(got[rows, mine_half], proj[which, mine_half], preferred_element_type=F32)
+            return 0
+
+        lax.fori_loop(0, 4, body, 0)
+
     def terms_of(which):
         def terms(i, _):
             z, x = turn_of(i)
             first = pl.multiple_of(x * 448 + z * 224, 32)
-            btf[0:224, :] = jnp.dot(got[pl.ds(first, 224), :], proj[which], preferred_element_type=F32)
+            rows = pl.ds(first, 224)
+            btf[0:224, :] = early[rows, :] + jnp.dot(got[rows, their_half], proj[which, their_half], preferred_element_type=F32)
             for k in range(4):
                 two = btf[56 * k : 56 * k + 64, :]
                 btb[which, 0, z, x * 4 + k] = two[:PAD].astype(BF16)
@@ -299,6 +312,7 @@
         return terms
 
     def make_terms(which):
+        early_terms(which)
         all_shared(which)
         lax.fori_loop(0, 8, terms_of(which), 0)
 
@@ -355,6 +369,7 @@
                 def _():
                     send_terms(which, z, q).start()
 
+        early_terms(which)
         all_shared(which)
         lax.fori_loop(0, 8 + BEHIND, body, 0)
 
@@ -424,9 +439,8 @@
     swap_sum(1 - zh).wait()
     grad_sub = to_natural(jnp.concatenate([total[h] + zrecv[h].astype(F32) for h in range(2)], axis=1))[:OWNED]
 
-    moment_new, second_new, direction = adam_direction(grad_sub, mom[...], sec[...])
-    mnew[...] = moment_new
-    snew[...] = second_new
+    _, _, direction = adam_direction(grad_sub, mom[...], sec[...])
+    grad[...] = grad_sub
     direct[OWNED - 4 :, :] = jnp.zeros((PAD - OWNED + 4, RANK), F32)
     direct[:OWNED, :] = to_halves(direction)
     dirs[f] = direct[...].astype(BF16)
@@ -487,15 +501,14 @@
     vmem = pl.BlockSpec(memory_space=pltpu.VMEM)
     anywhere = pl.BlockSpec(memory_space=pl.ANY)
     dma = pltpu.SemaphoreType.DMA
-    update, moment_new, second_new = pl.pallas_call(
+    update, grad_sub = pl.pallas_call(
         kernel,
         out_shape=(
             jax.ShapeDtypeStruct((OWNED * LINE, FEATURES), BF16),
             jax.ShapeDtypeStruct((OWNED, RANK), F32),
-            jax.ShapeDtypeStruct((OWNED, RANK), F32),
         ),
         in_specs=[anywhere, anywhere, anywhere, anywhere, anywhere],
-        out_specs=(vmem, vmem, vmem),
+        out_specs=(vmem, vmem),
         scratch_shapes=[
             pltpu.VMEM((TOKENS, FEATURES), BF16),
             pltpu.VMEM((TOKENS, UNITS), BF16),
@@ -512,6 +525,7 @@
             pltpu.VMEM((2, SHARE, 128), BF16),
             pltpu.VMEM((2, SHARE, 128), BF16),
             pltpu.VMEM((2, TOKENS, 128), BF16),
+            pltpu.VMEM((UNITS, 128), F32),
             pltpu.VMEM((232, 128), F32),
             pltpu.VMEM((2, 2, 2, 16, PAD, 128), BF16),
             pltpu.VMEM((2, 2, 16, PAD, 128), BF16),
@@ -535,6 +549,7 @@
         compiler_params=pltpu.CompilerParams(
             collective_id=0, has_side_effects=True, vmem_limit_bytes=48 * 1024 * 1024),
     )(*[pltpu.with_memory_space_constraint(v, pltpu.HBM) for v in (blk, inputs, grad_out, moment, second)])
+    moment_new, second_new, _ = adam_direction(grad_sub, moment, second)
     return (update.reshape(OWNED, LINE, FEATURES).transpose(1, 0, 2), moment_new, second_new)
 
 

time: 79.7 us -> 79.3 us (level)
  local copies, waits for them, and re-layouts: 2 us -> 0.78 us
  Pallas kernels: 75.7 us -> 76.5 us
    unnamed x3 -> x5, local copies, waits for them, and re-layouts: 2 us -> 0.78 us
where the time goes in v6:
time: 79.3 us; the launch traced here: 78.6 us
  Pallas kernels  76.5 us (96%)
    pallas_call x1, Pallas kernels, local(): pl.pallas_call(kernel, out_shape=(jax.ShapeDtypeStruct((OWNED * LINE, FEA...  76.5 us

profile of v6, /device:TPU:24, one launch (start us, length us, event | category | flops | bytes accessed | tf_op | source)
XLA Modules:
  0.0 78.6 jit_solution(15471411975587386504)
XLA Ops:
  0.6 0.0 copy-start.1
  0.6 0.0 copy-start
  0.7 76.5 %shard_map.76 = (bf16[224,1024]{1,0:T(8,128)(2,1)S(1)}, f32[28,256]{1,0:T(8,128)S(1)}) custom-call(bf16[32,128]{1,0:T(8,128)(2,1)} %bitcast.11, bf16[768,1024]{1,0:T(8,128)(2,1)} %x_hbm.1, bf16[768,1792]{1,0:T(8,128)(2,1)} %go_hbm.1, f32[28,256]{1,0:T(8,128)} %mom_hbm.1, f32[28,256]{1,0:T(8,128)} %sec_hbm.1), custom_call_target="tpu_custom_call" | custom-call | tf_op jit(solution)/shard_map/pallas_call | solution.py:504
  77.1 0.0 copy-done.1
  77.2 0.0 copy-done
  77.2 0.6 fusion
  77.8 0.8 copy.10
Async XLA Ops:
  0.6 76.5 %copy-start.1 = (f32[28,256]{1,0:T(8,128)S(1)}, f32[28,256]{1,0:T(8,128)}, u32[]{:S(2)}) copy-start(f32[28,256]{1,0:T(8,128)} %sec_hbm.1) | copy-start | bytes 86020
  0.6 76.5 %copy-start = (f32[28,256]{1,0:T(8,128)S(1)}, f32[28,256]{1,0:T(8,128)}, u32[]{:S(2)}) copy-start(f32[28,256]{1,0:T(8,128)} %mom_hbm.1) | copy-start | bytes 86020

commit v7 on v6

--- a/solution.py
+++ b/solution.py
@@ -456,7 +456,18 @@
             return 0
         lax.fori_loop(1, LINE, body, 0)
 
-    each_line(lambda i: send_dir(i).start())
+    down = (LINE - 1 - f) // (LINE // 2)
+
+    def start_dir(j, _):
+        q = j + down * (LINE - 1 - 2 * j)
+
+        @pl.when(q != f)
+        def _():
+            send_dir(lax.rem(q - f + LINE, LINE)).start()
+
+        return 0
+
+    lax.fori_loop(0, LINE, start_dir, 0)
 
     def wait_dir(i):
         q = lax.rem(f + LINE - i, LINE)

time: 79.3 us -> 79.2 us (level)
  no operation moved by 1% of the time
where the time goes in v7:
time: 79.2 us; the launch traced here: 78.6 us
  Pallas kernels  76.5 us (97%)
    pallas_call x1, Pallas kernels, local(): pl.pallas_call(kernel, out_shape=(jax.ShapeDtypeStruct((OWNED * LINE, FEA...  76.5 us

profile of v7, /device:TPU:24, one launch (start us, length us, event | category | flops | bytes accessed | tf_op | source)
XLA Modules:
  0.0 78.6 jit_solution(4240082466229720496)
XLA Ops:
  0.6 0.0 copy-start.1
  0.6 0.0 copy-start
  0.7 76.5 %shard_map.76 = (bf16[224,1024]{1,0:T(8,128)(2,1)S(1)}, f32[28,256]{1,0:T(8,128)S(1)}) custom-call(bf16[32,128]{1,0:T(8,128)(2,1)} %bitcast.11, bf16[768,1024]{1,0:T(8,128)(2,1)} %x_hbm.1, bf16[768,1792]{1,0:T(8,128)(2,1)} %go_hbm.1, f32[28,256]{1,0:T(8,128)} %mom_hbm.1, f32[28,256]{1,0:T(8,128)} %sec_hbm.1), custom_call_target="tpu_custom_call" | custom-call | tf_op jit(solution)/shard_map/pallas_call | solution.py:515
  77.1 0.0 copy-done.1
  77.1 0.0 copy-done
  77.1 0.6 fusion
  77.8 0.8 copy.10
Async XLA Ops:
  0.6 76.5 %copy-start.1 = (f32[28,256]{1,0:T(8,128)S(1)}, f32[28,256]{1,0:T(8,128)}, u32[]{:S(2)}) copy-start(f32[28,256]{1,0:T(8,128)} %sec_hbm.1) | copy-start | bytes 86020
  0.6 76.5 %copy-start = (f32[28,256]{1,0:T(8,128)S(1)}, f32[28,256]{1,0:T(8,128)}, u32[]{:S(2)}) copy-start(f32[28,256]{1,0:T(8,128)} %mom_hbm.1) | copy-start | bytes 86020
